TPU v7x, 32 devices: a whole 2x2x4 slice. The times are simulated.
32 devices in a mesh: chan: 4 (over x, core), region: 8 (over z, y).
Axes of the slice: x: 2, y: 2, z: 4, core: 2. Of those that a mesh axis runs over, the one named last changes fastest.
Arguments:
- latent: bfloat16 [8, 24, 24, 12, 128], P('region'), may hold values from -6 to 6
- cond_scale: float32 [128], replicated, may hold values from 0.5 to 1.5
- cond_shift: float32 [128], replicated, may hold values from -3 to 3
- fine_weight: bfloat16 [3, 3, 3, 128, 128], replicated, may hold values from -0.109375 to 0.109375
- fine_bias: float32 [128], replicated, may hold values from -3 to 3
- proj_weight: bfloat16 [8192, 1024], P(('chan', 'region')), may hold values from -0.0625 to 0.0625
- proj_bias: float32 [1024], replicated, may hold values from -3 to 3
- bottle_weight: bfloat16 [27, 1024, 1024], P(None, 'chan'), may hold values from -0.0390625 to 0.0390625
- bottle_bias: float32 [1024], replicated, may hold values from -3 to 3
- guide: float32 [1], replicated, may hold values from 1.5 to 4
Outputs:
- guided: bfloat16 [8, 6, 6, 3, 1024], P('region', None, None, None, 'chan')
All inputs are finite; a program needn't handle non-finite values.
Results may differ from a plain program's by a relative error of at most 0.012.
The roundings to bfloat16 on the way count: a program that leaves them out, or rounds other values in their place, can miss the bound.
Values may be sent and summed in bfloat16 or wider, within the bound.
No kernel may reach another device: no remote copies, remote signals or barrier semaphores. Data moves between devices by JAX's collectives and lax.ppermute only.
A program may use at most 128 MiB of HBM per device.

v0:
```python
import functools

import numpy as np

import jax
import jax.numpy as jnp
from jax import lax
from jax.experimental import pallas as pl
from jax.experimental.pallas import tpu as pltpu
from jax.sharding import PartitionSpec as P

FINE_WIDTH = 128
COARSE_WIDTH = 1024
TILE_SIDE = 12
STRIDE = 4
REGIONS_Y = 4
REGIONS_Z = 2

CELLS = TILE_SIDE // STRIDE
ACROSS = 2 * CELLS
PLANE = 2 * ACROSS * ACROSS
ROWS = CELLS * PLANE
PADDED = -(-ROWS // 16) * 16
PHASES = STRIDE + 2
OFFSETS = STRIDE**3
LANES = 128
SPREAD = 8
MIB = 2**20


def vmem(count):
    return [pl.BlockSpec(memory_space=pltpu.VMEM) for _ in range(count)]


def regroup_kernel(*refs):
    rows_refs, out_ref, wide = refs[:-2], refs[-2], refs[-1]
    held = rows_refs[0].shape[0]
    groups = out_ref.shape[1]
    for lane in range(wide.shape[0]):
        columns = slice(lane * LANES, (lane + 1) * LANES)
        for number, rows_ref in enumerate(rows_refs):
            wide[lane, number * held : (number + 1) * held, :] = rows_ref[:, columns].astype(jnp.float32)
        for offset in range(OFFSETS):
            out_ref[offset, :, columns] = wide[
                lane, pl.ds(offset, groups, stride=OFFSETS), :
            ].astype(jnp.bfloat16)


def regroup(pieces):
    held, width = pieces[0].shape
    total = len(pieces) * held
    return pl.pallas_call(
        regroup_kernel,
        out_shape=jax.ShapeDtypeStruct((OFFSETS, total // OFFSETS, width), jnp.bfloat16),
        in_specs=vmem(len(pieces)),
        out_specs=vmem(1)[0],
        scratch_shapes=[pltpu.VMEM((width // LANES, total, LANES), jnp.float32)],
        compiler_params=pltpu.CompilerParams(vmem_limit_bytes=8 * MIB),
        name="regroup",
    )(*pieces)


def split_kernel(place_ref, rows_ref, *out_refs):
    width = out_refs[0].shape[1]
    for distance, out_ref in enumerate(out_refs):
        start = pl.multiple_of((place_ref[0] ^ distance) * width, width)
        out_ref[...] = rows_ref[:, pl.ds(start, width)]


def split_columns(place, rows, owners):
    held, width = rows.shape[0], rows.shape[1] // owners
    return pl.pallas_call(
        split_kernel,
        out_shape=[jax.ShapeDtypeStruct((held, width), rows.dtype)] * owners,
        in_specs=[pl.BlockSpec(memory_space=pltpu.SMEM)] + vmem(1),
        out_specs=vmem(owners),
        compiler_params=pltpu.CompilerParams(vmem_limit_bytes=4 * MIB),
        name="split_columns",
    )(place, rows)


def rows_kernel(first_ref, last_ref, low_ref, high_ref, wide):
    def take(at_x, carry):
        for rows_ref, row, out_ref in ((first_ref, 0, low_ref), (last_ref, 7, high_ref)):
            for at_z in range(TILE_SIDE):
                wide[at_z : at_z + 1, :] = rows_ref[at_x, at_z].astype(jnp.float32)[row : row + 1]
            out_ref[at_x] = wide[...].astype(jnp.bfloat16)
        return carry

    wide[...] = jnp.zeros_like(wide)
    lax.fori_loop(0, first_ref.shape[0], take, 0)


def y_rows(block):
    side_x, depth, side_y, width = block.shape
    return pl.pallas_call(
        rows_kernel,
        out_shape=(
            jax.ShapeDtypeStruct((side_x, 16, width), block.dtype),
            jax.ShapeDtypeStruct((side_x, 16, width), block.dtype),
        ),
        grid=(1,),
        in_specs=[
            pl.BlockSpec((side_x, depth, 8, width), lambda i: (0, 0, 0, 0)),
            pl.BlockSpec((side_x, depth, 8, width), lambda i: (0, 0, side_y // 8 - 1, 0)),
        ],
        out_specs=(
            pl.BlockSpec((side_x, 16, width), lambda i: (0, 0, 0)),
            pl.BlockSpec((side_x, 16, width), lambda i: (0, 0, 0)),
        ),
        scratch_shapes=[pltpu.VMEM((16, width), jnp.float32)],
        compiler_params=pltpu.CompilerParams(vmem_limit_bytes=12 * MIB),
        name="y_rows",
    )(block, block)


def window_kernel(
    inside_ref, block_ref, layer_ref, below_ref, above_ref, outer_ref, scale_ref, shift_ref,
    weight_ref, order_ref, windows_ref, taps_ref, rows, line, layers,
):
    phase_x = pl.program_id(0)
    side, depth, width = 2 * TILE_SIDE, TILE_SIDE, FINE_WIDTH
    half = 2 * ACROSS * side

    @pl.when(phase_x == 0)
    def _():
        zero = jnp.zeros((width, width), jnp.bfloat16)
        for place in range(9):
            taps_ref[place, 3 * width :, :width] = zero
            taps_ref[place, :width, width:] = zero
            for step in range(3):
                block = jnp.dot(
                    weight_ref[place * 3 + step], order_ref[...], preferred_element_type=jnp.float32
                ).astype(jnp.bfloat16)
                taps_ref[place, step * width : (step + 1) * width, :width] = block
                taps_ref[place, (step + 1) * width : (step + 2) * width, width:] = block

        def widen(at_x, carry):
            rows[0, at_x] = below_ref[at_x].astype(jnp.float32)
            rows[1, at_x] = above_ref[at_x].astype(jnp.float32)
            return carry

        lax.fori_loop(0, side, widen, 0)

    scale = jnp.broadcast_to(scale_ref[...], (8, width))
    shift = jnp.broadcast_to(shift_ref[...], (8, width))
    row = lax.broadcasted_iota(jnp.int32, (8, width), 0)
    first = jnp.where(row == 0, shift * inside_ref[2], shift)
    last = jnp.where(row == side + 1 - 20, shift * inside_ref[3], shift)
    chunks = [(0, first), (8, shift), (16, shift), (4, shift), (12, shift), (20, last)]

    def split(cell_x, carry):
        at_x = phase_x + STRIDE * cell_x
        outside = jnp.logical_or(at_x == 0, at_x == side + 1)

        @pl.when(jnp.logical_not(outside))
        def _():
            at = at_x - 1
            for at_z in range(depth + 2):
                if at_z == 0:
                    flag, value, place = inside_ref[4], layer_ref[at], depth
                elif at_z == depth + 1:
                    flag, value, place = inside_ref[5], layer_ref[at], depth
                else:
                    flag, value, place = None, block_ref[at, at_z - 1], at_z - 1
                value = value.astype(jnp.float32)
                low, high = rows[0, at, place : place + 1, :], rows[1, at, place : place + 1, :]
                if flag is not None:
                    value, low, high = value * flag, low * flag, high * flag
                line[at_z, 7:8, :] = low
                line[at_z, 8 : side + 8, :] = value
                line[at_z, side + 8 : side + 9, :] = high

        @pl.when(outside)
        def _():
            end = jnp.where(at_x == 0, 0, 1)
            for at_z in range(depth + 2):
                value = outer_ref[end, at_z].astype(jnp.float32)
                line[at_z, 0:8, :] = value[side : side + 8]
                line[at_z, 8 : side + 8, :] = value[:side]
                line[at_z, side + 8 : side + 16, :] = value[side : side + 8]

        within = jnp.where(at_x == 0, inside_ref[0], 1.0)
        within = jnp.where(at_x == side + 1, inside_ref[1], within)
        for at_z in range(depth + 2):
            if at_z == 0:
                factor = within * inside_ref[4]
            elif at_z == depth + 1:
                factor = within * inside_ref[5]
            else:
                factor = within
            for number, (start, added) in enumerate(chunks):
                value = line[at_z, pl.ds(start + 7, 8), :]
                base = number // 3 * half + number % 3 * 8
                base = pl.multiple_of(base + cell_x * side, 8)
                layers[at_z, pl.ds(base, 8), :] = value
                layers[at_z, pl.ds(base + half // 2, 8), :] = value * scale + added * factor
        return carry

    lax.fori_loop(0, ACROSS, split, 0)
    for phase_y in range(PHASES):
        start = phase_y if phase_y < STRIDE else half + phase_y - STRIDE
        for phase_z in range(PHASES):
            parts = [
                layers[phase_z + STRIDE * cell, pl.ds(start, PLANE, stride=STRIDE), :]
                for cell in range(CELLS)
            ]
            parts.append(jnp.zeros((PADDED - ROWS, width), jnp.float32))
            windows_ref[0, phase_y, :, phase_z * width : (phase_z + 1) * width] = jnp.concatenate(
                parts, axis=0
            ).astype(jnp.bfloat16)


def make_windows(inside, *arrays):
    width, side = FINE_WIDTH, 2 * TILE_SIDE

    def whole(array):
        return pl.BlockSpec(array.shape, lambda i: (0,) * array.ndim)

    return pl.pallas_call(
        window_kernel,
        out_shape=(
            jax.ShapeDtypeStruct((PHASES, PHASES, PADDED, PHASES * width), jnp.bfloat16),
            jax.ShapeDtypeStruct((9, 4 * width, 2 * width), jnp.bfloat16),
        ),
        grid=(PHASES,),
        in_specs=[pl.BlockSpec(memory_space=pltpu.SMEM)] + [whole(array) for array in arrays],
        out_specs=(
            pl.BlockSpec((1, PHASES, PADDED, PHASES * width), lambda i: (i, 0, 0, 0)),
            pl.BlockSpec((9, 4 * width, 2 * width), lambda i: (0, 0, 0)),
        ),
        scratch_shapes=[
            pltpu.VMEM((2, side, 16, width), jnp.float32),
            pltpu.VMEM((TILE_SIDE + 2, side + 16, width), jnp.float32),
            pltpu.VMEM((TILE_SIDE + 2, 4 * ACROSS * side, width), jnp.float32),
        ],
        compiler_params=pltpu.CompilerParams(vmem_limit_bytes=28 * MIB),
        cost_estimate=pl.CostEstimate(flops=10**10, bytes_accessed=16 * MIB, transcendentals=0),
        name="windows",
    )(inside, *arrays)


def convolve_kernel(first_ref, second_ref, third_ref, taps_ref, bias_ref, out_ref):
    width = FINE_WIDTH
    bias = bias_ref[...]

    def convolve(at_y, carry):
        total = jnp.zeros((2 * PADDED, 2 * width), jnp.float32)
        for step_x, windows_ref in enumerate((first_ref, second_ref, third_ref)):
            for step_y in range(3):
                taken = [
                    windows_ref[0, at_y + step_y, :, pair * 2 * width : (pair * 2 + 4) * width]
                    for pair in range(2)
                ]
                total += jnp.dot(
                    jnp.concatenate(taken, axis=0),
                    taps_ref[step_x * 3 + step_y],
                    preferred_element_type=jnp.float32,
                )
        total = total + bias
        hidden = (total / (1.0 + jnp.exp(-total))).astype(jnp.bfloat16)
        for pair in range(2):
            out_ref[at_y * 2 + pair] = hidden[pair * PADDED : (pair + 1) * PADDED]
        return carry

    lax.fori_loop(0, STRIDE, convolve, 0)


def convolve(windows, taps, bias, start, count):
    width = FINE_WIDTH
    each = STRIDE * STRIDE // 2
    block = (1, PHASES, PADDED, PHASES * width)
    return pl.pallas_call(
        convolve_kernel,
        out_shape=jax.ShapeDtypeStruct((count * each, PADDED, 2 * width), jnp.bfloat16),
        grid=(count,),
        in_specs=[
            pl.BlockSpec(block, lambda i, step=step: (i + start + step, 0, 0, 0)) for step in range(3)
        ]
        + [
            pl.BlockSpec(taps.shape, lambda i: (0, 0, 0)),
            pl.BlockSpec(bias.shape, lambda i: (0, 0)),
        ],
        out_specs=pl.BlockSpec((each, PADDED, 2 * width), lambda i: (i, 0, 0)),
        compiler_params=pltpu.CompilerParams(vmem_limit_bytes=28 * MIB),
        cost_estimate=pl.CostEstimate(
            flops=2 * count * each * PADDED * 36 * width * 2 * width,
            bytes_accessed=16 * MIB,
            transcendentals=count * each * PADDED * 2 * width,
        ),
        name="convolve",
    )(windows, windows, windows, taps, bias)


def project_kernel(split, place_ref, early_ref, late_ref, *refs):
    weight_refs, bias_ref, out_ref = refs[:-2], refs[-2], refs[-1]
    width = out_ref.shape[1]
    start = pl.multiple_of(place_ref[0] * width, width)
    total = jnp.broadcast_to(bias_ref[:, pl.ds(start, width)], out_ref.shape)
    pairs = early_ref.shape[0]
    for number, hidden_ref in enumerate((early_ref, late_ref)):
        used = weight_refs[:-2] + (weight_refs[len(weight_refs) - 2 + number],) if split else weight_refs
        for pair in range(pairs):
            weight = jnp.concatenate(
                [
                    ref[2 * pair + item + (number * 2 * pairs if ref.shape[0] == OFFSETS else 0)]
                    for item in range(2)
                    for ref in used
                ],
                axis=0,
            )
            total += jnp.dot(hidden_ref[pair], weight, preferred_element_type=jnp.float32)
    out_ref[...] = total.astype(jnp.bfloat16)


def project(place, early, late, weights, split, bias):
    pairs, rows, depth = early.shape
    width = weights[0].shape[2]
    return pl.pallas_call(
        functools.partial(project_kernel, split),
        out_shape=jax.ShapeDtypeStruct((rows, width), jnp.bfloat16),
        in_specs=[pl.BlockSpec(memory_space=pltpu.SMEM)] + vmem(len(weights) + 3),
        out_specs=vmem(1)[0],
        compiler_params=pltpu.CompilerParams(vmem_limit_bytes=24 * MIB),
        cost_estimate=pl.CostEstimate(
            flops=4 * pairs * rows * depth * width, bytes_accessed=8 * MIB, transcendentals=0
        ),
        name="project",
    )(place, early, late, *weights, bias)


def bottle_kernel(far, place_ref, field_ref, weight_ref, *refs):
    out_refs, (held, total, packed, dense, sems) = refs[:-5], refs[-5:]
    width = field_ref.shape[4]
    share = out_refs[0].shape[1]
    span = held.shape[2]
    frame = ACROSS + 2
    rows = CELLS * 2 * ACROSS * frame
    chunk = 256
    owners = 2 * len(out_refs)
    first = pl.multiple_of((place_ref[0] // len(out_refs) ^ far) * span, span)

    def copy_of(step_y, place):
        tap = (place // 3 * 3 + step_y) * 3 + place % 3
        return pltpu.make_async_copy(
            weight_ref.at[tap, :, pl.ds(first, span)],
            held.at[step_y, pl.ds(place * width, width)],
            sems.at[step_y, place],
        )

    for step_y in range(3):
        for place in range(9):
            copy_of(step_y, place).start()

    for step_x in range(3):
        for step_z in range(3):
            place = step_x * 3 + step_z
            packed[:, place * width : (place + 1) * width] = (
                field_ref[step_z : step_z + CELLS, :, step_x : step_x + ACROSS]
                .astype(jnp.float32)
                .reshape(rows, width)
                .astype(jnp.bfloat16)
            )

    for step_x in range(3):
        for step_z in range(3):
            copy_of(0, step_x * 3 + step_z).wait()
        depth = slice(step_x * 3 * width, (step_x + 1) * 3 * width)
        for start in range(0, span, chunk):
            columns = slice(start, start + chunk)
            terms = jnp.dot(
                packed[:, depth], held[0, depth, columns], preferred_element_type=jnp.float32
            )
            total[0, :, columns] = terms if step_x == 0 else total[0, :, columns] + terms

    def rest(step_y, carry):
        for place in range(9):
            copy_of(step_y, place).wait()
        for start in range(0, span, chunk):
            columns = slice(start, start + chunk)
            total[step_y, :, columns] = jnp.dot(
                packed[...], held[step_y, :, columns], preferred_element_type=jnp.float32
            )
        return carry

    lax.fori_loop(1, 3, rest, 0)

    for number, out_ref in enumerate(out_refs):
        distance = number + far * owners // 2
        start = pl.multiple_of((place_ref[0] ^ distance) % len(out_refs) * share, share)
        for group in range(rows // frame):
            at = group * frame
            dense[group * ACROSS : (group + 1) * ACROSS, :] = sum(
                total[item, at + item : at + item + ACROSS, pl.ds(start, share)]
                for item in range(3)
            )
        out_ref[...] = dense[...].astype(out_ref.dtype)


def bottle_terms(place, field, weight, owners, far):
    frame = ACROSS + 2
    rows = CELLS * 2 * ACROSS * frame
    width = weight.shape[1]
    share = COARSE_WIDTH // owners
    span = COARSE_WIDTH // 2
    return pl.pallas_call(
        functools.partial(bottle_kernel, int(far)),
        out_shape=[
            jax.ShapeDtypeStruct((ROWS, share), jnp.bfloat16 if far or number else jnp.float32)
            for number in range(owners // 2)
        ],
        in_specs=[
            pl.BlockSpec(memory_space=pltpu.SMEM),
            pl.BlockSpec(memory_space=pltpu.VMEM),
            pl.BlockSpec(memory_space=pltpu.HBM),
        ],
        out_specs=vmem(owners // 2),
        scratch_shapes=[
            pltpu.VMEM((3, 9 * width, span), jnp.bfloat16),
            pltpu.VMEM((3, rows, span), jnp.float32),
            pltpu.VMEM((rows, 9 * width), jnp.bfloat16),
            pltpu.VMEM((ROWS, share), jnp.float32),
            pltpu.SemaphoreType.DMA((3, 9)),
        ],
        compiler_params=pltpu.CompilerParams(vmem_limit_bytes=51 * MIB),
        cost_estimate=pl.CostEstimate(
            flops=2 * rows * 27 * width * span, bytes_accessed=8 * MIB, transcendentals=0
        ),
        name="bottle_far" if far else "bottle_near",
    )(place, field, weight)


def finish_kernel(place_ref, guide_ref, own_ref, *refs):
    other_refs, bias_ref, out_ref, spread = refs[:-3], refs[-3], refs[-2], refs[-1]
    share = own_ref.shape[1]
    start = pl.multiple_of(place_ref[0] * share, share)
    value = own_ref[...] + bias_ref[:, pl.ds(start, share)]
    for other_ref in other_refs:
        value = value + other_ref[...].astype(jnp.float32)
    value = value / (1.0 + jnp.exp(-value))
    half = PLANE // 2
    for cell in range(CELLS):
        plain = value[cell * PLANE : cell * PLANE + half]
        guided = value[cell * PLANE + half : (cell + 1) * PLANE]
        mixed = plain + guide_ref[0] * (guided - plain)
        for lane in range(spread.shape[0]):
            spread[lane, pl.ds(cell, half, stride=SPREAD), :] = mixed[:, lane * LANES : (lane + 1) * LANES]
    for lane in range(spread.shape[0]):
        for cell in range(half):
            out_ref[cell, :, lane * LANES : (lane + 1) * LANES] = spread[
                lane, cell * SPREAD : cell * SPREAD + CELLS, :
            ].astype(jnp.bfloat16)


def finish(place, guide, terms, bias):
    share = terms[0].shape[1]
    return pl.pallas_call(
        finish_kernel,
        out_shape=jax.ShapeDtypeStruct((PLANE // 2, CELLS, share), jnp.bfloat16),
        in_specs=[pl.BlockSpec(memory_space=pltpu.SMEM)] * 2 + vmem(len(terms) + 1),
        out_specs=vmem(1)[0],
        scratch_shapes=[pltpu.VMEM((share // LANES, PLANE // 2 * SPREAD, LANES), jnp.float32)],
        compiler_params=pltpu.CompilerParams(vmem_limit_bytes=8 * MIB),
        name="finish",
    )(place, guide, *terms, bias)


def passed(value, steps):
    count = lax.axis_size("region")
    return lax.ppermute(
        value, "region", [(at, at + steps) for at in range(max(0, -steps), min(count, count - steps))]
    )


def across_z(value):
    count = lax.axis_size("region")
    return lax.ppermute(value, "region", [(at, at ^ 1) for at in range(count)])


def y_halos(first, last):
    place = lax.axis_index("region") // REGIONS_Z % REGIONS_Y
    upper = is_upper()
    ahead = hop(jnp.where(upper, first, last), True)
    back = hop(jnp.where(upper, last, first), False)
    zero = jnp.zeros_like(ahead)
    below = jnp.where(place > 0, jnp.where(upper, back, ahead), zero)
    above = jnp.where(place < REGIONS_Y - 1, jnp.where(upper, ahead, back), zero)
    return below, above


def with_halos(value, dim_x, dim_y, dim_z):
    value = jnp.concatenate(z_ends(z_layer(value, dim_z), value, dim_z), axis=dim_z)
    below, above = y_halos(edge(value, dim_y, False), edge(value, dim_y, True))
    value = jnp.concatenate([below, value, above], axis=dim_y)
    low, high = x_layers(edge(value, dim_x, False), edge(value, dim_x, True))
    return jnp.concatenate([low, value, high], axis=dim_x)


def edge(array, dim, last):
    size = array.shape[dim]
    return lax.slice_in_dim(array, size - 1 if last else 0, size if last else 1, axis=dim)


def is_upper():
    return lax.axis_index("region") % REGIONS_Z == 1


def z_layer(value, dim):
    return across_z(jnp.where(is_upper(), edge(value, dim, False), edge(value, dim, True)))


def z_ends(layer, value, dim):
    zero = jnp.zeros_like(layer)
    return [jnp.where(is_upper(), layer, zero), value, jnp.where(is_upper(), zero, layer)]


def x_layers(first, last):
    count = lax.axis_size("region") // (REGIONS_Y * REGIONS_Z)
    if count == 1:
        return jnp.zeros_like(last), jnp.zeros_like(first)
    return passed(last, REGIONS_Y * REGIONS_Z), passed(first, -REGIONS_Y * REGIONS_Z)


def chan_swap(value, distance):
    return lax.ppermute(value, "chan", [(at, at ^ distance) for at in range(lax.axis_size("chan"))])


def exchange(piece_at):
    chans = lax.axis_size("chan")
    return [piece_at(0)] + [chan_swap(piece_at(distance), distance) for distance in range(1, chans)]


def ring_of(count):
    return list(range(0, count, 2)) + list(range(1, count, 2))[::-1]


def hop(value, ahead):
    ring = ring_of(lax.axis_size("region"))
    following = ring[1:] + ring[:1]
    return lax.ppermute(value, "region", list(zip(ring, following) if ahead else zip(following, ring)))


def after(value, other):
    return lax.optimization_barrier((value, other))[0]


def piece_channels(each):
    chans, regions = lax.axis_size("chan"), lax.axis_size("region")
    ring = ring_of(regions)
    shifts = [0]
    for step in range(1, regions // 2 + 1):
        shifts += [-step] + [step] * (step < regions // 2)
    origin = np.array(
        [[ring[(ring.index(region) + shift) % regions] for shift in shifts] for region in range(regions)]
    )
    table = np.zeros((chans, regions, regions, chans, each), np.int32)
    for chan in range(chans):
        for distance in range(chans):
            first = (chan ^ distance) * regions + origin
            table[chan, :, :, distance] = first[:, :, None] * each + np.arange(each)
    table = jnp.asarray(table.reshape(chans * regions, FINE_WIDTH))
    device = lax.axis_index("chan") * regions + lax.axis_index("region")
    return lax.dynamic_index_in_dim(table, device, 0, keepdims=True)


def ring_pieces(piece, milestones):
    regions = lax.axis_size("region")
    forward = backward = piece
    held = [piece]
    for step in range(1, regions // 2 + 1):
        if step > 1 and step - 2 < len(milestones):
            forward, backward = (after(value, milestones[step - 2]) for value in (forward, backward))
        if step == regions // 2:
            held += [hop(forward[: OFFSETS // 2], True), hop(backward[OFFSETS // 2 :], False)]
        else:
            forward, backward = hop(forward, True), hop(backward, False)
            held += [forward, backward]
    return held


def whole_columns(proj_weight):
    chans, held = lax.axis_size("chan"), proj_weight.shape[0]
    width = COARSE_WIDTH // chans
    mine = lax.all_to_all(proj_weight, "chan", split_axis=1, concat_axis=0, tiled=True)
    whole = lax.all_gather(mine.reshape(chans, held, width), "region", axis=1, tiled=True)
    return whole.reshape(FINE_WIDTH, OFFSETS, width).transpose(1, 0, 2)


def shards(
    latent,
    cond_scale,
    cond_shift,
    fine_weight,
    fine_bias,
    proj_weight,
    proj_bias,
    bottle_weight,
    bottle_bias,
    guide,
):
    chans = lax.axis_size("chan")
    chan_place = lax.axis_index("chan")
    region = lax.axis_index("region")
    width = COARSE_WIDTH // chans
    side = 2 * TILE_SIDE
    count_x = lax.axis_size("region") // (REGIONS_Y * REGIONS_Z)
    steps = (REGIONS_Y * REGIONS_Z, REGIONS_Z, 1)
    counts = (count_x, REGIONS_Y, REGIONS_Z)
    places = [region // step % count for step, count in zip(steps, counts)]
    inside = jnp.stack(
        [
            flag
            for place, count in zip(places, counts)
            for flag in ((place > 0).astype(jnp.float32), (place < count - 1).astype(jnp.float32))
        ]
    )

    place = chan_place[None]
    each, rest = divmod(proj_weight.shape[0], OFFSETS)
    by_ring = rest == 0 and chans * each % 16 == 0
    if by_ring:
        split = split_columns(place, proj_weight, chans)
        mine = exchange(lambda distance: split[distance])
        piece = regroup(mine)
        channel = piece_channels(each)
    else:
        channel = jnp.arange(FINE_WIDTH, dtype=jnp.int32)[None]
    order = lax.broadcasted_iota(jnp.int32, (FINE_WIDTH, FINE_WIDTH), 0) == channel

    block = latent[0].transpose(0, 2, 1, 3)
    face = lax.dynamic_index_in_dim(
        block, jnp.where(is_upper(), 0, TILE_SIDE - 1), axis=1, keepdims=False
    )
    first, last = y_rows(block)
    layer = across_z(face)
    corner = lax.broadcasted_iota(jnp.int32, first.shape, 1) == TILE_SIDE
    below, above = y_halos(
        jnp.where(corner, layer[:, :1], first), jnp.where(corner, layer[:, -1:], last)
    )
    ends = []
    for at in (0, -1):
        plane = jnp.concatenate(z_ends(layer[at][None], block[at], 0), axis=0)
        low, high = [
            jnp.concatenate(
                z_ends(part[at, TILE_SIDE : TILE_SIDE + 1], part[at, :TILE_SIDE], 0), axis=0
            )[:, None]
            for part in (below, above)
        ]
        spare = jnp.zeros((TILE_SIDE + 2, 6, FINE_WIDTH), plane.dtype)
        ends.append(jnp.concatenate([plane, high, spare, low], axis=1))
    outer = jnp.stack(x_layers(*ends))

    bias = jnp.sum(jnp.where(order, fine_bias[:, None], 0.0), axis=0)
    windows, taps = make_windows(
        inside,
        block,
        layer,
        below,
        above,
        outer,
        cond_scale[None],
        cond_shift[None],
        fine_weight.reshape(27, FINE_WIDTH, FINE_WIDTH),
        order.astype(jnp.bfloat16),
    )
    bias = jnp.concatenate([bias, bias])[None]
    half = STRIDE // 2
    early = convolve(windows, taps, bias, 0, half)
    late = convolve(windows, taps, bias, half, half)
    columns = ring_pieces(piece, [taps, early, late]) if by_ring else [whole_columns(proj_weight)]
    coarse = project(place, early, late, columns, by_ring, proj_bias[None])

    grid = coarse[:ROWS].reshape(CELLS, 2, ACROSS, ACROSS, width)
    field = with_halos(grid, 2, 3, 0)
    far = bottle_terms(place, field, bottle_weight, chans, True)
    swapped = [chan_swap(value, chans // 2 + number) for number, value in enumerate(far)]
    own, *near = bottle_terms(after(place, far), field, bottle_weight, chans, False)
    near = [chan_swap(value, 1 + number) for number, value in enumerate(near)]
    terms = [own, sum(value.astype(jnp.float32) for value in swapped)] + near
    guided = finish(place, guide, terms, bottle_bias[None])
    return guided.reshape(1, ACROSS, ACROSS, CELLS, width)


def solution(mesh):
    placed = (
        P("region", None, None, None, None),
        P(),
        P(),
        P(),
        P(),
        P(("chan", "region"), None),
        P(),
        P(None, "chan", None),
        P(),
        P(),
    )
    return jax.shard_map(
        shards,
        mesh=mesh,
        in_specs=placed,
        out_specs=P("region", None, None, None, "chan"),
        check_vma=False,
    )
```

profile of v0, /device:TPU:0, one launch (start us, length us, event | category | flops | bytes accessed | tf_op | source)
XLA Modules:
  0.0 86.0 jit_solution(1742744545233116828)
XLA Ops:
  0.0 0.9 %dynamic-slice_bitcast_fusion = bf16[24,24,128]{2,1,0:T(8,128)(2,1)S(1)} fusion(bf16[1,24,24,12,128]{4,2,3,1,0:T(8,128)(2,1)} %param.11, s32[]{:T(128)S(6)} %select_n.158), kind=kLoop, calls=%fused_computation.2 | loop fusion | bytes 294916 | tf_op jit(solution)/shard_map/jit(dynamic_index_in_dim)/squeeze | solution.py:631
  0.9 3.0 %collective-permute-start = (bf16[24,24,128]{2,1,0:T(8,128)(2,1)S(1)}, bf16[24,24,128]{2,1,0:T(8,128)(2,1)S(1)}, u32[]{:S(2)}, u32[]{:S(2)}) collective-permute-start(bf16[24,24,128]{2,1,0:T(8,128)(2,1)S(1)} %dynamic-slice_bitcast_fusion), channel_id=1, source_target_pairs={{0,1},{1,0},{2,3},{3,2},{4,5},{5,4},{6,7},{7,6},{8,9},{9,8},{10,11... | collective-permute-start | bytes 442376 | tf_op jit(solution)/shard_map/ppermute | solution.py:477
  4.0 1.0 %copy-done.2 = bf16[256,1024]{1,0:T(8,128)(2,1)S(1)} copy-done((bf16[256,1024]{1,0:T(8,128)(2,1)S(1)}, bf16[256,1024]{1,0:T(8,128)(2,1)}, u32[]{:S(2)}) %copy-start.2) | copy-done | bytes 524312
  5.0 0.1 split_columns.1
  5.1 0.0 copy-start.8
  5.1 0.1 collective-permute-start.3
  5.2 1.6 %collective-permute-start.4 = (bf16[256,256]{1,0:T(8,128)(2,1)S(1)}, bf16[256,256]{1,0:T(8,128)(2,1)S(1)}, u32[]{:S(2)}, u32[]{:S(2)}) collective-permute-start(bf16[256,256]{1,0:T(8,128)(2,1)S(1)} %get-tuple-element.30), channel_id=1, source_target_pairs={{0,16},{8,24},{16,0},{24,8},{1,17},{9,25},{17,1},{25,9},{2,18},{10... | collective-permute-start | bytes 393224 | tf_op jit(solution)/shard_map/ppermute | solution.py:525
  6.7 0.3 collective-permute-start.5
  7.0 0.7 dynamic-slice_bitcast_fusion.1
  7.8 0.1 stack.30
  7.9 1.5 %copy-done = bf16[1,24,24,12,128]{4,2,3,1,0:T(8,128)(2,1)S(1)} copy-done((bf16[1,24,24,12,128]{4,2,3,1,0:T(8,128)(2,1)S(1)}, bf16[1,24,24,12,128]{4,2,3,1,0:T(8,128)(2,1)}, u32[]{:S(2)}) %copy-start) | copy-done | bytes 1769496
  9.4 0.7 y_rows.1
  10.1 0.0 copy-start.1
  10.1 0.0 copy-start.6
  10.1 0.0 copy-start.7
  10.1 0.1 select_reduce_fusion
  10.2 0.0 collective-permute-done.layer_ref
  10.2 0.1 broadcast_select_fusion.8
  10.3 1.6 %collective-permute-start.2 = (bf16[24,16,128]{2,1,0:T(8,128)(2,1)S(1)}, bf16[24,16,128]{2,1,0:T(8,128)(2,1)S(1)}, u32[]{:S(2)}, u32[]{:S(2)}) collective-permute-start(bf16[24,16,128]{2,1,0:T(8,128)(2,1)S(1)} %get-tuple-element.46), channel_id=1, source_target_pairs={{0,2},{2,4},{4,6},{6,7},{7,5},{5,3},{3,1},{1,0},{8,10},{10,12},{12... | collective-permute-start | bytes 294920 | tf_op jit(solution)/shard_map/ppermute | solution.py:540
  12.0 0.4 collective-permute-start.1
  12.4 0.0 collective-permute-done.3.refs_1_
  12.4 0.0 collective-permute-done.4.refs_2_
  12.4 1.0 %collective-permute-done.5.refs_3_ = bf16[256,256]{1,0:T(8,128)(2,1)S(1)} collective-permute-done((bf16[256,256]{1,0:T(8,128)(2,1)S(1)}, bf16[256,256]{1,0:T(8,128)(2,1)S(1)}, u32[]{:S(2)}, u32[]{:S(2)}) %collective-permute-start.5) | collective-permute-done | bytes 131104 | tf_op jit(solution)/shard_map/ppermute | solution.py:525
  13.4 0.7 regroup.1.refs_0_
  14.1 1.6 %collective-permute-start.6 = (bf16[64,16,256]{2,1,0:T(8,128)(2,1)S(1)}, bf16[64,16,256]{2,1,0:T(8,128)(2,1)S(1)}, u32[]{:S(2)}, u32[]{:S(2)}) collective-permute-start(bf16[64,16,256]{2,1,0:T(8,128)(2,1)S(1)} %regroup.1.refs_0_), channel_id=1, source_target_pairs={{0,2},{2,4},{4,6},{6,7},{7,5},{5,3},{3,1},{1,0},{8,10},{10,12},{12... | collective-permute-start | bytes 1572872 | tf_op jit(solution)/shard_map/ppermute | solution.py:540
  15.7 0.4 collective-permute-start.7
  16.2 0.5 collective-permute-done.1
  16.8 6.1 %windows.1 = (bf16[6,6,224,768]{3,2,1,0:T(8,128)(2,1)S(1)}, bf16[9,512,256]{2,1,0:T(8,128)(2,1)S(1)}) custom-call(f32[6]{0:T(128)S(1)} %stack.31.inside_ref, bf16[24,12,24,128]{3,2,1,0:T(8,128)(2,1)S(1)} %bitcast.25, bf16[24,24,128]{2,1,0:T(8,128)(2,1)S(1)} %collective-permute-done.layer_ref, bf16[24,16,128]{2,1,0:T(8,128)(2,1)S(1)} %get-tuple-element.49.below_ref, ...), custom_call_target="tpu_custom_call" | custom-call | flops 10000000000 | bytes 16777216 | tf_op jit(solution)/shard_map/windows/pallas_call | solution.py:220
  22.9 5.3 %collective-permute-done.6.refs_1_ = bf16[64,16,256]{2,1,0:T(8,128)(2,1)S(1)} collective-permute-done((bf16[64,16,256]{2,1,0:T(8,128)(2,1)S(1)}, bf16[64,16,256]{2,1,0:T(8,128)(2,1)S(1)}, u32[]{:S(2)}, u32[]{:S(2)}) %collective-permute-start.6) | collective-permute-done | bytes 524320 | tf_op jit(solution)/shard_map/ppermute | solution.py:540
  28.3 1.6 %collective-permute-start.8 = (bf16[64,16,256]{2,1,0:T(8,128)(2,1)S(1)}, bf16[64,16,256]{2,1,0:T(8,128)(2,1)S(1)}, u32[]{:S(2)}, u32[]{:S(2)}) collective-permute-start(bf16[64,16,256]{2,1,0:T(8,128)(2,1)S(1)} %collective-permute-done.6.refs_1_), channel_id=1, source_target_pairs={{0,2},{2,4},{4,6},{6,7},{7,5},{5,3},{3,1},{1,0},{8,10},{10,12},{12... | collective-permute-start | bytes 1572872 | tf_op jit(solution)/shard_map/ppermute | solution.py:540
  29.8 0.0 collective-permute-done.7.refs_2_
  29.9 0.5 collective-permute-start.9
  30.3 10.1 %convolve.2.early_ref = bf16[16,224,256]{2,1,0:T(8,128)(2,1)S(1)} custom-call(bf16[6,6,224,768]{3,2,1,0:T(8,128)(2,1)S(1)} %get-tuple-element.26.first_ref.second_ref.third_ref, bf16[6,6,224,768]{3,2,1,0:T(8,128)(2,1)S(1)} %get-tuple-element.26.first_ref.second_ref.third_ref, bf16[6,6,224,768]{3,2,1,0:T(8,128)(2,1)S(1)} %get-tuple-element.26.first_ref.second_ref.third_ref, ...), custom_call_target="tpu_custom_call" | custom-call | flops 8455716864 | bytes 16777216 | tf_op jit(solution)/shard_map/convolve/pallas_call | solution.py:273
  40.4 0.0 copy-start.3
  40.4 1.1 %collective-permute-done.8.refs_3_ = bf16[64,16,256]{2,1,0:T(8,128)(2,1)S(1)} collective-permute-done((bf16[64,16,256]{2,1,0:T(8,128)(2,1)S(1)}, bf16[64,16,256]{2,1,0:T(8,128)(2,1)S(1)}, u32[]{:S(2)}, u32[]{:S(2)}) %collective-permute-start.8) | collective-permute-done | bytes 524320 | tf_op jit(solution)/shard_map/ppermute | solution.py:540
  41.6 1.6 %collective-permute-start.10 = (bf16[64,16,256]{2,1,0:T(8,128)(2,1)S(1)}, bf16[64,16,256]{2,1,0:T(8,128)(2,1)S(1)}, u32[]{:S(2)}, u32[]{:S(2)}) collective-permute-start(bf16[64,16,256]{2,1,0:T(8,128)(2,1)S(1)} %collective-permute-done.8.refs_3_), channel_id=1, source_target_pairs={{0,2},{2,4},{4,6},{6,7},{7,5},{5,3},{3,1},{1,0},{8,10},{10,12},{12... | collective-permute-start | bytes 1572872 | tf_op jit(solution)/shard_map/ppermute | solution.py:540
  43.1 0.0 collective-permute-done.9.refs_4_
  43.1 0.5 collective-permute-start.11
  43.6 10.1 %convolve.3.late_ref = bf16[16,224,256]{2,1,0:T(8,128)(2,1)S(1)} custom-call(bf16[6,6,224,768]{3,2,1,0:T(8,128)(2,1)S(1)} %get-tuple-element.26.first_ref.second_ref.third_ref, bf16[6,6,224,768]{3,2,1,0:T(8,128)(2,1)S(1)} %get-tuple-element.26.first_ref.second_ref.third_ref, bf16[6,6,224,768]{3,2,1,0:T(8,128)(2,1)S(1)} %get-tuple-element.26.first_ref.second_ref.third_ref, ...), custom_call_target="tpu_custom_call" | custom-call | flops 8455716864 | bytes 16777216 | tf_op jit(solution)/shard_map/convolve/pallas_call | solution.py:273
  53.7 0.2 collective-permute-done.10.refs_5_
  54.0 1.6 %collective-permute-start.12 = (bf16[32,16,256]{2,1,0:T(8,128)(2,1)S(1)}, bf16[32,16,256]{2,1,0:T(8,128)(2,1)S(1)}, u32[]{:S(2)}, u32[]{:S(2)}) collective-permute-start(bf16[32,16,256]{2,1,0:T(8,128)(2,1)S(1)} %slice.33), channel_id=1, source_target_pairs={{0,2},{2,4},{4,6},{6,7},{7,5},{5,3},{3,1},{1,0},{8,10},{10,12},{12... | collective-permute-start | bytes 786440 | tf_op jit(solution)/shard_map/ppermute | solution.py:540
  55.6 0.5 collective-permute-start.13
  56.1 4.3 %collective-permute-done.12.refs_7_ = bf16[32,16,256]{2,1,0:T(8,128)(2,1)S(1)} collective-permute-done((bf16[32,16,256]{2,1,0:T(8,128)(2,1)S(1)}, bf16[32,16,256]{2,1,0:T(8,128)(2,1)S(1)}, u32[]{:S(2)}, u32[]{:S(2)}) %collective-permute-start.12) | collective-permute-done | bytes 262176 | tf_op jit(solution)/shard_map/ppermute | solution.py:540
  60.4 1.7 %collective-permute-done.13.refs_8_ = bf16[32,16,256]{2,1,0:T(8,128)(2,1)S(1)} collective-permute-done((bf16[32,16,256]{2,1,0:T(8,128)(2,1)S(1)}, bf16[32,16,256]{2,1,0:T(8,128)(2,1)S(1)}, u32[]{:S(2)}, u32[]{:S(2)}) %collective-permute-start.13) | collective-permute-done | bytes 262176 | tf_op jit(solution)/shard_map/ppermute | solution.py:540
  62.0 1.1 %project.1 = bf16[224,256]{1,0:T(8,128)(2,1)S(1)} custom-call(s32[1]{0:T(128)} %bitcast.place_ref, bf16[16,224,256]{2,1,0:T(8,128)(2,1)S(1)} %convolve.2.early_ref, bf16[16,224,256]{2,1,0:T(8,128)(2,1)S(1)} %convolve.3.late_ref, bf16[64,16,256]{2,1,0:T(8,128)(2,1)S(1)} %regroup.1.refs_0_, bf16[64,16,256]{2,1,0:T(8,128)(2,1)S(1)} %collective-permute-done.6.refs_1_, ...), custom_call_target="tpu_custom_call" | custom-call | flops 939524096 | bytes 8388608 | tf_op jit(solution)/shard_map/project/pallas_call | solution.py:319
  63.2 0.5 collective-permute-start.14
  63.8 3.6 %collective-permute-done.14 = bf16[1,2,6,6,256]{4,3,2,1,0:T(8,128)(2,1)S(1)} collective-permute-done((bf16[1,2,6,6,256]{4,3,2,1,0:T(8,128)(2,1)S(1)}, bf16[1,2,6,6,256]{4,3,2,1,0:T(8,128)(2,1)S(1)}, u32[]{:S(2)}, u32[]{:S(2)}) %collective-permute-start.14) | collective-permute-done | bytes 36896 | tf_op jit(solution)/shard_map/ppermute | solution.py:477
  67.4 0.1 broadcast_select_fusion.4
  67.5 0.5 collective-permute-start.15
  68.0 0.1 broadcast_select_fusion.3
  68.1 1.6 %collective-permute-start.16 = (bf16[5,2,6,1,256]{4,3,2,1,0:T(2,128)(2,1)S(1)}, bf16[5,2,6,1,256]{4,3,2,1,0:T(2,128)(2,1)S(1)}, u32[]{:S(2)}, u32[]{:S(2)}) collective-permute-start(bf16[5,2,6,1,256]{4,3,2,1,0:T(2,128)(2,1)S(1)} %broadcast_select_fusion.3), channel_id=1, source_target_pairs={{0,2},{2,4},{4,6},{6,7},{7,5},{5,3},{3,1},{1,0},{8,10},{10,12},{12... | collective-permute-start | bytes 92168 | tf_op jit(solution)/shard_map/ppermute | solution.py:540
  70.4 1.4 %collective-permute-done.15 = bf16[5,2,6,1,256]{4,3,2,1,0:T(2,128)(2,1)S(1)} collective-permute-done((bf16[5,2,6,1,256]{4,3,2,1,0:T(2,128)(2,1)S(1)}, bf16[5,2,6,1,256]{4,3,2,1,0:T(2,128)(2,1)S(1)}, u32[]{:S(2)}, u32[]{:S(2)}) %collective-permute-start.15) | collective-permute-done | bytes 30752 | tf_op jit(solution)/shard_map/ppermute | solution.py:540
  71.8 0.6 collective-permute-done.16
  72.4 0.1 broadcast_select_fusion.5
  72.6 0.2 pad_maximum_fusion.field_ref
  72.8 4.5 %bottle_far.1 = (bf16[216,256]{1,0:T(8,128)(2,1)S(1)}, bf16[216,256]{1,0:T(8,128)(2,1)S(1)}) custom-call(s32[1]{0:T(128)} %bitcast.place_ref, bf16[5,2,8,8,256]{4,3,2,1,0:T(8,128)(2,1)S(1)} %pad_maximum_fusion.field_ref, bf16[27,256,1024]{2,1,0:T(8,128)(2,1)} %weight_ref.3), custom_call_target="tpu_custom_call" | custom-call | flops 2038431744 | bytes 8388608 | tf_op jit(solution)/shard_map/bottle_far/pallas_call | solution.py:406
  77.3 0.1 collective-permute-start.18
  77.4 0.0 copy-start.4
  77.4 1.6 %collective-permute-start.17 = (bf16[216,256]{1,0:T(8,128)(2,1)S(1)}, bf16[216,256]{1,0:T(8,128)(2,1)S(1)}, u32[]{:S(2)}, u32[]{:S(2)}) collective-permute-start(bf16[216,256]{1,0:T(8,128)(2,1)S(1)} %get-tuple-element.38), channel_id=1, source_target_pairs={{0,16},{8,24},{16,0},{24,8},{1,17},{9,25},{17,1},{25,9},{2,18},{10... | collective-permute-start | bytes 331784 | tf_op jit(solution)/shard_map/ppermute | solution.py:525
  79.0 4.6 %bottle_near.1 = (f32[216,256]{1,0:T(8,128)S(1)}, bf16[216,256]{1,0:T(8,128)(2,1)S(1)}) custom-call(s32[1]{0:T(128)} %bitcast.place_ref, bf16[5,2,8,8,256]{4,3,2,1,0:T(8,128)(2,1)S(1)} %pad_maximum_fusion.field_ref, bf16[27,256,1024]{2,1,0:T(8,128)(2,1)} %weight_ref.3), custom_call_target="tpu_custom_call" | custom-call | flops 2038431744 | bytes 8388608 | tf_op jit(solution)/shard_map/bottle_near/pallas_call | solution.py:406
  83.7 0.3 collective-permute-start.19
  83.9 1.2 %collective-permute-done.17 = bf16[216,256]{1,0:T(8,128)(2,1)S(1)} collective-permute-done((bf16[216,256]{1,0:T(8,128)(2,1)S(1)}, bf16[216,256]{1,0:T(8,128)(2,1)S(1)}, u32[]{:S(2)}, u32[]{:S(2)}) %collective-permute-start.17) | collective-permute-done | bytes 110624 | tf_op jit(solution)/shard_map/ppermute | solution.py:525
  85.1 0.0 collective-permute-done.19.refs_1_
  85.2 0.8 finish.1
  (30 shorter events, 0.3 us)
Async XLA Ops:
  0.9 9.3 %collective-permute-start = (bf16[24,24,128]{2,1,0:T(8,128)(2,1)S(1)}, bf16[24,24,128]{2,1,0:T(8,128)(2,1)S(1)}, u32[]{:S(2)}, u32[]{:S(2)}) collective-permute-start(bf16[24,24,128]{2,1,0:T(8,128)(2,1)S(1)} %dynamic-slice_bitcast_fusion), channel_id=1, source_target_pairs={{0,1},{1,0},{2,3},{3,2},{4,5},{5,4},{6,7},{7,6},{8,9},{9,8},{10,11... | collective-permute-start | bytes 442376 | tf_op jit(solution)/shard_map/ppermute | solution.py:477
  4.0 1.0 %copy-start.2 = (bf16[256,1024]{1,0:T(8,128)(2,1)S(1)}, bf16[256,1024]{1,0:T(8,128)(2,1)}, u32[]{:S(2)}) copy-start(bf16[256,1024]{1,0:T(8,128)(2,1)} %rows_ref.1) | copy-start | bytes 1572868
  5.1 5.0 %copy-start.8 = (f32[128]{0:T(128)S(1)}, f32[128]{0:T(128)}, u32[]{:S(2)}) copy-start(f32[128]{0:T(128)} %param.15) | copy-start | bytes 1540
  5.1 7.3 %collective-permute-start.3 = (bf16[256,256]{1,0:T(8,128)(2,1)S(1)}, bf16[256,256]{1,0:T(8,128)(2,1)S(1)}, u32[]{:S(2)}, u32[]{:S(2)}) collective-permute-start(bf16[256,256]{1,0:T(8,128)(2,1)S(1)} %get-tuple-element.29), channel_id=1, source_target_pairs={{0,8},{8,0},{16,24},{24,16},{1,9},{9,1},{17,25},{25,17},{2,10},{10... | collective-permute-start | bytes 393224 | tf_op jit(solution)/shard_map/ppermute | solution.py:525
  5.2 7.3 %collective-permute-start.4 = (bf16[256,256]{1,0:T(8,128)(2,1)S(1)}, bf16[256,256]{1,0:T(8,128)(2,1)S(1)}, u32[]{:S(2)}, u32[]{:S(2)}) collective-permute-start(bf16[256,256]{1,0:T(8,128)(2,1)S(1)} %get-tuple-element.30), channel_id=1, source_target_pairs={{0,16},{8,24},{16,0},{24,8},{1,17},{9,25},{17,1},{25,9},{2,18},{10... | collective-permute-start | bytes 393224 | tf_op jit(solution)/shard_map/ppermute | solution.py:525
  6.7 6.7 %collective-permute-start.5 = (bf16[256,256]{1,0:T(8,128)(2,1)S(1)}, bf16[256,256]{1,0:T(8,128)(2,1)S(1)}, u32[]{:S(2)}, u32[]{:S(2)}) collective-permute-start(bf16[256,256]{1,0:T(8,128)(2,1)S(1)} %get-tuple-element.31), channel_id=1, source_target_pairs={{0,24},{8,16},{16,8},{24,0},{1,25},{9,17},{17,9},{25,1},{2,26},{10... | collective-permute-start | bytes 393224 | tf_op jit(solution)/shard_map/ppermute | solution.py:525
  7.9 1.5 %copy-start = (bf16[1,24,24,12,128]{4,2,3,1,0:T(8,128)(2,1)S(1)}, bf16[1,24,24,12,128]{4,2,3,1,0:T(8,128)(2,1)}, u32[]{:S(2)}) copy-start(bf16[1,24,24,12,128]{4,2,3,1,0:T(8,128)(2,1)} %param.11) | copy-start | bytes 5308420
  9.4 7.4 %copy-start.5 = (bf16[3,3,3,128,128]{4,3,2,1,0:T(8,128)(2,1)S(1)}, bf16[3,3,3,128,128]{4,3,2,1,0:T(8,128)(2,1)}, u32[]{:S(2)}) copy-start(bf16[3,3,3,128,128]{4,3,2,1,0:T(8,128)(2,1)} %param.14) | copy-start | bytes 2654212
  10.1 6.8 %copy-start.1 = (bf16[1,24,24,12,128]{4,2,3,1,0:T(8,128)(2,1)S(1)}, bf16[1,24,24,12,128]{4,2,3,1,0:T(8,128)(2,1)}, u32[]{:S(2)}) copy-start(bf16[1,24,24,12,128]{4,2,3,1,0:T(8,128)(2,1)} %param.11) | copy-start | bytes 5308420
  10.1 6.8 %copy-start.6 = (f32[128]{0:T(128)S(1)}, f32[128]{0:T(128)}, u32[]{:S(2)}) copy-start(f32[128]{0:T(128)} %param.12) | copy-start | bytes 1540
  10.1 6.8 %copy-start.7 = (f32[128]{0:T(128)S(1)}, f32[128]{0:T(128)}, u32[]{:S(2)}) copy-start(f32[128]{0:T(128)} %param.13) | copy-start | bytes 1540
  10.3 5.9 %collective-permute-start.2 = (bf16[24,16,128]{2,1,0:T(8,128)(2,1)S(1)}, bf16[24,16,128]{2,1,0:T(8,128)(2,1)S(1)}, u32[]{:S(2)}, u32[]{:S(2)}) collective-permute-start(bf16[24,16,128]{2,1,0:T(8,128)(2,1)S(1)} %get-tuple-element.46), channel_id=1, source_target_pairs={{0,2},{2,4},{4,6},{6,7},{7,5},{5,3},{3,1},{1,0},{8,10},{10,12},{12... | collective-permute-start | bytes 294920 | tf_op jit(solution)/shard_map/ppermute | solution.py:540
  12.0 4.8 %collective-permute-start.1 = (bf16[24,16,128]{2,1,0:T(8,128)(2,1)S(1)}, bf16[24,16,128]{2,1,0:T(8,128)(2,1)S(1)}, u32[]{:S(2)}, u32[]{:S(2)}) collective-permute-start(bf16[24,16,128]{2,1,0:T(8,128)(2,1)S(1)} %get-tuple-element.47), channel_id=1, source_target_pairs={{2,0},{4,2},{6,4},{7,6},{5,7},{3,5},{1,3},{0,1},{10,8},{12,10},{14... | collective-permute-start | bytes 294920 | tf_op jit(solution)/shard_map/ppermute | solution.py:540
  14.1 14.2 %collective-permute-start.6 = (bf16[64,16,256]{2,1,0:T(8,128)(2,1)S(1)}, bf16[64,16,256]{2,1,0:T(8,128)(2,1)S(1)}, u32[]{:S(2)}, u32[]{:S(2)}) collective-permute-start(bf16[64,16,256]{2,1,0:T(8,128)(2,1)S(1)} %regroup.1.refs_0_), channel_id=1, source_target_pairs={{0,2},{2,4},{4,6},{6,7},{7,5},{5,3},{3,1},{1,0},{8,10},{10,12},{12... | collective-permute-start | bytes 1572872 | tf_op jit(solution)/shard_map/ppermute | solution.py:540
  15.7 14.1 %collective-permute-start.7 = (bf16[64,16,256]{2,1,0:T(8,128)(2,1)S(1)}, bf16[64,16,256]{2,1,0:T(8,128)(2,1)S(1)}, u32[]{:S(2)}, u32[]{:S(2)}) collective-permute-start(bf16[64,16,256]{2,1,0:T(8,128)(2,1)S(1)} %regroup.1.refs_0_), channel_id=1, source_target_pairs={{2,0},{4,2},{6,4},{7,6},{5,7},{3,5},{1,3},{0,1},{10,8},{12,10},{14... | collective-permute-start | bytes 1572872 | tf_op jit(solution)/shard_map/ppermute | solution.py:540
  28.3 13.3 %collective-permute-start.8 = (bf16[64,16,256]{2,1,0:T(8,128)(2,1)S(1)}, bf16[64,16,256]{2,1,0:T(8,128)(2,1)S(1)}, u32[]{:S(2)}, u32[]{:S(2)}) collective-permute-start(bf16[64,16,256]{2,1,0:T(8,128)(2,1)S(1)} %collective-permute-done.6.refs_1_), channel_id=1, source_target_pairs={{0,2},{2,4},{4,6},{6,7},{7,5},{5,3},{3,1},{1,0},{8,10},{10,12},{12... | collective-permute-start | bytes 1572872 | tf_op jit(solution)/shard_map/ppermute | solution.py:540
  29.9 13.3 %collective-permute-start.9 = (bf16[64,16,256]{2,1,0:T(8,128)(2,1)S(1)}, bf16[64,16,256]{2,1,0:T(8,128)(2,1)S(1)}, u32[]{:S(2)}, u32[]{:S(2)}) collective-permute-start(bf16[64,16,256]{2,1,0:T(8,128)(2,1)S(1)} %collective-permute-done.7.refs_2_), channel_id=1, source_target_pairs={{2,0},{4,2},{6,4},{7,6},{5,7},{3,5},{1,3},{0,1},{10,8},{12,10},{14... | collective-permute-start | bytes 1572872 | tf_op jit(solution)/shard_map/ppermute | solution.py:540
  40.4 21.6 %copy-start.3 = (f32[1024]{0:T(1024)S(1)}, f32[1024]{0:T(1024)}, u32[]{:S(2)}) copy-start(f32[1024]{0:T(1024)} %param.17) | copy-start | bytes 12292
  41.6 12.4 %collective-permute-start.10 = (bf16[64,16,256]{2,1,0:T(8,128)(2,1)S(1)}, bf16[64,16,256]{2,1,0:T(8,128)(2,1)S(1)}, u32[]{:S(2)}, u32[]{:S(2)}) collective-permute-start(bf16[64,16,256]{2,1,0:T(8,128)(2,1)S(1)} %collective-permute-done.8.refs_3_), channel_id=1, source_target_pairs={{0,2},{2,4},{4,6},{6,7},{7,5},{5,3},{3,1},{1,0},{8,10},{10,12},{12... | collective-permute-start | bytes 1572872 | tf_op jit(solution)/shard_map/ppermute | solution.py:540
  43.1 12.4 %collective-permute-start.11 = (bf16[64,16,256]{2,1,0:T(8,128)(2,1)S(1)}, bf16[64,16,256]{2,1,0:T(8,128)(2,1)S(1)}, u32[]{:S(2)}, u32[]{:S(2)}) collective-permute-start(bf16[64,16,256]{2,1,0:T(8,128)(2,1)S(1)} %collective-permute-done.9.refs_4_), channel_id=1, source_target_pairs={{2,0},{4,2},{6,4},{7,6},{5,7},{3,5},{1,3},{0,1},{10,8},{12,10},{14... | collective-permute-start | bytes 1572872 | tf_op jit(solution)/shard_map/ppermute | solution.py:540
  54.0 6.4 %collective-permute-start.12 = (bf16[32,16,256]{2,1,0:T(8,128)(2,1)S(1)}, bf16[32,16,256]{2,1,0:T(8,128)(2,1)S(1)}, u32[]{:S(2)}, u32[]{:S(2)}) collective-permute-start(bf16[32,16,256]{2,1,0:T(8,128)(2,1)S(1)} %slice.33), channel_id=1, source_target_pairs={{0,2},{2,4},{4,6},{6,7},{7,5},{5,3},{3,1},{1,0},{8,10},{10,12},{12... | collective-permute-start | bytes 786440 | tf_op jit(solution)/shard_map/ppermute | solution.py:540
  55.6 6.4 %collective-permute-start.13 = (bf16[32,16,256]{2,1,0:T(8,128)(2,1)S(1)}, bf16[32,16,256]{2,1,0:T(8,128)(2,1)S(1)}, u32[]{:S(2)}, u32[]{:S(2)}) collective-permute-start(bf16[32,16,256]{2,1,0:T(8,128)(2,1)S(1)} %slice.34), channel_id=1, source_target_pairs={{2,0},{4,2},{6,4},{7,6},{5,7},{3,5},{1,3},{0,1},{10,8},{12,10},{14... | collective-permute-start | bytes 786440 | tf_op jit(solution)/shard_map/ppermute | solution.py:540
  63.2 4.2 %collective-permute-start.14 = (bf16[1,2,6,6,256]{4,3,2,1,0:T(8,128)(2,1)S(1)}, bf16[1,2,6,6,256]{4,3,2,1,0:T(8,128)(2,1)S(1)}, u32[]{:S(2)}, u32[]{:S(2)}) collective-permute-start(bf16[1,2,6,6,256]{4,3,2,1,0:T(8,128)(2,1)S(1)} %select_n.173), channel_id=1, source_target_pairs={{0,1},{1,0},{2,3},{3,2},{4,5},{5,4},{6,7},{7,6},{8,9},{9,8},{10,11... | collective-permute-start | bytes 110600 | tf_op jit(solution)/shard_map/ppermute | solution.py:477
  67.5 4.3 %collective-permute-start.15 = (bf16[5,2,6,1,256]{4,3,2,1,0:T(2,128)(2,1)S(1)}, bf16[5,2,6,1,256]{4,3,2,1,0:T(2,128)(2,1)S(1)}, u32[]{:S(2)}, u32[]{:S(2)}) collective-permute-start(bf16[5,2,6,1,256]{4,3,2,1,0:T(2,128)(2,1)S(1)} %get-tuple-element.43), channel_id=1, source_target_pairs={{2,0},{4,2},{6,4},{7,6},{5,7},{3,5},{1,3},{0,1},{10,8},{12,10},{14... | collective-permute-start | bytes 92168 | tf_op jit(solution)/shard_map/ppermute | solution.py:540
  68.1 4.3 %collective-permute-start.16 = (bf16[5,2,6,1,256]{4,3,2,1,0:T(2,128)(2,1)S(1)}, bf16[5,2,6,1,256]{4,3,2,1,0:T(2,128)(2,1)S(1)}, u32[]{:S(2)}, u32[]{:S(2)}) collective-permute-start(bf16[5,2,6,1,256]{4,3,2,1,0:T(2,128)(2,1)S(1)} %broadcast_select_fusion.3), channel_id=1, source_target_pairs={{0,2},{2,4},{4,6},{6,7},{7,5},{5,3},{3,1},{1,0},{8,10},{10,12},{12... | collective-permute-start | bytes 92168 | tf_op jit(solution)/shard_map/ppermute | solution.py:540
  77.3 6.6 %collective-permute-start.18 = (bf16[216,256]{1,0:T(8,128)(2,1)S(1)}, bf16[216,256]{1,0:T(8,128)(2,1)S(1)}, u32[]{:S(2)}, u32[]{:S(2)}) collective-permute-start(bf16[216,256]{1,0:T(8,128)(2,1)S(1)} %get-tuple-element.39), channel_id=1, source_target_pairs={{0,24},{8,16},{16,8},{24,0},{1,25},{9,17},{17,9},{25,1},{2,26},{10... | collective-permute-start | bytes 331784 | tf_op jit(solution)/shard_map/ppermute | solution.py:525
  77.4 7.8 %copy-start.4 = (f32[1024]{0:T(1024)S(1)}, f32[1024]{0:T(1024)}, u32[]{:S(2)}) copy-start(f32[1024]{0:T(1024)} %param.19) | copy-start | bytes 12292
  77.4 7.7 %collective-permute-start.17 = (bf16[216,256]{1,0:T(8,128)(2,1)S(1)}, bf16[216,256]{1,0:T(8,128)(2,1)S(1)}, u32[]{:S(2)}, u32[]{:S(2)}) collective-permute-start(bf16[216,256]{1,0:T(8,128)(2,1)S(1)} %get-tuple-element.38), channel_id=1, source_target_pairs={{0,16},{8,24},{16,0},{24,8},{1,17},{9,25},{17,1},{25,9},{2,18},{10... | collective-permute-start | bytes 331784 | tf_op jit(solution)/shard_map/ppermute | solution.py:525
  83.7 1.5 %collective-permute-start.19 = (bf16[216,256]{1,0:T(8,128)(2,1)S(1)}, bf16[216,256]{1,0:T(8,128)(2,1)S(1)}, u32[]{:S(2)}, u32[]{:S(2)}) collective-permute-start(bf16[216,256]{1,0:T(8,128)(2,1)S(1)} %get-tuple-element.42), channel_id=1, source_target_pairs={{0,8},{8,0},{16,24},{24,16},{1,9},{9,1},{17,25},{25,17},{2,10},{10... | collective-permute-start | bytes 331784 | tf_op jit(solution)/shard_map/ppermute | solution.py:525
where the time goes:
time: 86.2 us; the launch traced here: 86 us
  Pallas kernels  38.7 us (45%)
  waiting for transfers between devices  21 us (24%)
  starting transfers between devices  19.9 us (23%)
  local copies, waits for them, and re-layouts  4.46 us (5%)
  between operations  1.01 us (1%)
  other arithmetic  0.89 us (1%)
    pallas_call x2, Pallas kernels, convolve(): pl.pallas_call(convolve_kernel, out_shape=jax.ShapeDtypeStruct((count * e...  20.2 us
    ppermute x12, waiting for transfers between devices, hop(): lax.ppermute(value, 'region', list(zip(ring, following) if ahead else zip...  15.2 us
    ppermute x12, starting transfers between devices, hop(): lax.ppermute(value, 'region', list(zip(ring, following) if ahead else zip...  12.5 us
    pallas_call x2, Pallas kernels, bottle_terms(): pl.pallas_call(functools.partial(bottle_kernel, int(far)), out_shape=[jax...  9.12 us
    pallas_call x1, Pallas kernels, make_windows(): pl.pallas_call(window_kernel, out_shape=(jax.ShapeDtypeStruct((PHASES, PH...  6.09 us
    ppermute x6, starting transfers between devices, chan_swap(): lax.ppermute(value, 'chan', [(at, at ^ distance) for at in range(lax.axis...  3.91 us
    ppermute x2, waiting for transfers between devices, across_z(): return lax.ppermute(value, 'region', [(at, at ^ 1) for at in range(count)])  3.58 us
    ppermute x2, starting transfers between devices, across_z(): return lax.ppermute(value, 'region', [(at, at ^ 1) for at in range(count)])  3.55 us
  transfers between devices with their start and end apart: 20, of which 11 were waited for; matrix products, arithmetic and copies ran while one was open for 2% of the time, Pallas kernels for 38%

commit v1 on v0

--- a/solution.py
+++ b/solution.py
@@ -628,9 +628,10 @@
     order = lax.broadcasted_iota(jnp.int32, (FINE_WIDTH, FINE_WIDTH), 0) == channel
 
     block = latent[0].transpose(0, 2, 1, 3)
-    face = lax.dynamic_index_in_dim(
-        block, jnp.where(is_upper(), 0, TILE_SIDE - 1), axis=1, keepdims=False
-    )
+    outermost = jnp.where(is_upper(), 0, TILE_SIDE - 1)
+    if by_ring:
+        outermost = after(outermost, mine[1])
+    face = lax.dynamic_index_in_dim(block, outermost, axis=1, keepdims=False)
     first, last = y_rows(block)
     layer = across_z(face)
     corner = lax.broadcasted_iota(jnp.int32, first.shape, 1) == TILE_SIDE

time: 86.2 us -> 84.9 us (0.985)
  waiting for transfers between devices: 21 us -> 19.8 us
    ppermute x12, waiting for transfers between devices: 15.2 us -> 12.8 us  [hop(): lax.ppermute(value, 'region', list(zip(ring, following) if ahead else zip...]
    ppermute x2, waiting for transfers between devices: 3.58 us -> 5.76 us  [across_z(): return lax.ppermute(value, 'region', [(at, at ^ 1) for at in range(count)])]
    ppermute x2, starting transfers between devices: 3.55 us -> 2.12 us  [across_z(): return lax.ppermute(value, 'region', [(at, at ^ 1) for at in range(count)])]
    ppermute x6, starting transfers between devices: 3.91 us -> 5.18 us  [chan_swap(): lax.ppermute(value, 'chan', [(at, at ^ distance) for at in range(lax.axis...]
    ppermute x6, waiting for transfers between devices: 2.19 us -> 1.26 us  [chan_swap(): lax.ppermute(value, 'chan', [(at, at ^ distance) for at in range(lax.axis...]
  transfers between devices with their start and end apart: 20 -> 20, of which waited for: 11 -> 10; matrix products, arithmetic and copies ran while one was open for 2% -> 3% of each run, Pallas kernels for 38% -> 38%
where the time goes in v1:
time: 84.9 us; the launch traced here: 84.7 us
  Pallas kernels  38.7 us (46%)
  starting transfers between devices  19.8 us (23%)
  waiting for transfers between devices  19.8 us (23%)
  local copies, waits for them, and re-layouts  4.47 us (5%)
  between operations  0.95 us (1%)
  other arithmetic  0.89 us (1%)
    pallas_call x2, Pallas kernels, convolve(): pl.pallas_call(convolve_kernel, out_shape=jax.ShapeDtypeStruct((count * e...  20.2 us
    ppermute x12, waiting for transfers between devices, hop(): lax.ppermute(value, 'region', list(zip(ring, following) if ahead else zip...  12.8 us
    ppermute x12, starting transfers between devices, hop(): lax.ppermute(value, 'region', list(zip(ring, following) if ahead else zip...  12.5 us
    pallas_call x2, Pallas kernels, bottle_terms(): pl.pallas_call(functools.partial(bottle_kernel, int(far)), out_shape=[jax...  9.12 us
    pallas_call x1, Pallas kernels, make_windows(): pl.pallas_call(window_kernel, out_shape=(jax.ShapeDtypeStruct((PHASES, PH...  6.08 us
    ppermute x2, waiting for transfers between devices, across_z(): return lax.ppermute(value, 'region', [(at, at ^ 1) for at in range(count)])  5.76 us
    ppermute x6, starting transfers between devices, chan_swap(): lax.ppermute(value, 'chan', [(at, at ^ distance) for at in range(lax.axis...  5.18 us
    unnamed x19, local copies, waits for them, and re-layouts  2.57 us
  transfers between devices with their start and end apart: 20, of which 10 were waited for; matrix products, arithmetic and copies ran while one was open for 3% of the time, Pallas kernels for 38%

profile of v1, /device:TPU:0, one launch (start us, length us, event | category | flops | bytes accessed | tf_op | source)
XLA Modules:
  0.0 84.7 jit_solution(1087487521978991715)
XLA Ops:
  0.0 1.0 %copy-done.2 = bf16[256,1024]{1,0:T(8,128)(2,1)S(1)} copy-done((bf16[256,1024]{1,0:T(8,128)(2,1)S(1)}, bf16[256,1024]{1,0:T(8,128)(2,1)}, u32[]{:S(2)}) %copy-start.2) | copy-done | bytes 524312
  1.0 0.1 split_columns.1
  1.1 0.5 collective-permute-start
  1.6 2.6 %collective-permute-start.4 = (bf16[256,256]{1,0:T(8,128)(2,1)S(1)}, bf16[256,256]{1,0:T(8,128)(2,1)S(1)}, u32[]{:S(2)}, u32[]{:S(2)}) collective-permute-start(bf16[256,256]{1,0:T(8,128)(2,1)S(1)} %get-tuple-element.32), channel_id=1, source_target_pairs={{0,16},{8,24},{16,0},{24,8},{1,17},{9,25},{17,1},{25,9},{2,18},{10... | collective-permute-start | bytes 393224 | tf_op jit(solution)/shard_map/ppermute | solution.py:525
  4.2 0.1 collective-permute-start.5
  4.3 0.7 dynamic-slice_bitcast_fusion.1
  5.0 0.0 collective-permute-done.refs_1_
  5.0 0.9 %dynamic-slice_bitcast_fusion = bf16[24,24,128]{2,1,0:T(8,128)(2,1)S(1)} fusion(bf16[1,24,24,12,128]{4,2,3,1,0:T(8,128)(2,1)} %param.11, s32[]{:T(128)S(6)} %select_n.161), kind=kLoop, calls=%fused_computation.2 | loop fusion | bytes 294916 | tf_op jit(solution)/shard_map/jit(dynamic_index_in_dim)/squeeze | solution.py:634
  5.9 0.0 copy-start.8
  5.9 1.8 %collective-permute-start.1 = (bf16[24,24,128]{2,1,0:T(8,128)(2,1)S(1)}, bf16[24,24,128]{2,1,0:T(8,128)(2,1)S(1)}, u32[]{:S(2)}, u32[]{:S(2)}) collective-permute-start(bf16[24,24,128]{2,1,0:T(8,128)(2,1)S(1)} %dynamic-slice_bitcast_fusion), channel_id=1, source_target_pairs={{0,1},{1,0},{2,3},{3,2},{4,5},{5,4},{6,7},{7,6},{8,9},{9,8},{10,11... | collective-permute-start | bytes 442376 | tf_op jit(solution)/shard_map/ppermute | solution.py:477
  7.8 0.1 stack.30
  7.9 1.5 %copy-done = bf16[1,24,24,12,128]{4,2,3,1,0:T(8,128)(2,1)S(1)} copy-done((bf16[1,24,24,12,128]{4,2,3,1,0:T(8,128)(2,1)S(1)}, bf16[1,24,24,12,128]{4,2,3,1,0:T(8,128)(2,1)}, u32[]{:S(2)}) %copy-start) | copy-done | bytes 1769496
  9.4 0.7 y_rows.1
  10.0 0.0 copy-start.1
  10.0 0.0 copy-start.6
  10.1 0.0 copy-start.7
  10.1 0.1 select_reduce_fusion
  10.2 2.0 %collective-permute-done.1.layer_ref = bf16[24,24,128]{2,1,0:T(8,128)(2,1)S(1)} collective-permute-done((bf16[24,24,128]{2,1,0:T(8,128)(2,1)S(1)}, bf16[24,24,128]{2,1,0:T(8,128)(2,1)S(1)}, u32[]{:S(2)}, u32[]{:S(2)}) %collective-permute-start.1) | collective-permute-done | bytes 147488 | tf_op jit(solution)/shard_map/ppermute | solution.py:477
  12.2 0.1 broadcast_select_fusion.8
  12.3 1.8 %collective-permute-start.3 = (bf16[24,16,128]{2,1,0:T(8,128)(2,1)S(1)}, bf16[24,16,128]{2,1,0:T(8,128)(2,1)S(1)}, u32[]{:S(2)}, u32[]{:S(2)}) collective-permute-start(bf16[24,16,128]{2,1,0:T(8,128)(2,1)S(1)} %get-tuple-element.48), channel_id=1, source_target_pairs={{0,2},{2,4},{4,6},{6,7},{7,5},{5,3},{3,1},{1,0},{8,10},{10,12},{12... | collective-permute-start | bytes 294920 | tf_op jit(solution)/shard_map/ppermute | solution.py:540
  14.1 0.2 collective-permute-start.2
  14.3 0.0 collective-permute-done.4.refs_2_
  14.4 0.7 regroup.1.refs_0_
  15.0 1.8 %collective-permute-start.6 = (bf16[64,16,256]{2,1,0:T(8,128)(2,1)S(1)}, bf16[64,16,256]{2,1,0:T(8,128)(2,1)S(1)}, u32[]{:S(2)}, u32[]{:S(2)}) collective-permute-start(bf16[64,16,256]{2,1,0:T(8,128)(2,1)S(1)} %regroup.1.refs_0_), channel_id=1, source_target_pairs={{0,2},{2,4},{4,6},{6,7},{7,5},{5,3},{3,1},{1,0},{8,10},{10,12},{12... | collective-permute-start | bytes 1572872 | tf_op jit(solution)/shard_map/ppermute | solution.py:540
  16.9 0.2 collective-permute-start.7
  17.1 0.0 collective-permute-done.3
  17.1 2.2 %collective-permute-done.2 = bf16[24,16,128]{2,1,0:T(8,128)(2,1)S(1)} collective-permute-done((bf16[24,16,128]{2,1,0:T(8,128)(2,1)S(1)}, bf16[24,16,128]{2,1,0:T(8,128)(2,1)S(1)}, u32[]{:S(2)}, u32[]{:S(2)}) %collective-permute-start.2) | collective-permute-done | bytes 98336 | tf_op jit(solution)/shard_map/ppermute | solution.py:540
  19.4 6.1 %windows.1 = (bf16[6,6,224,768]{3,2,1,0:T(8,128)(2,1)S(1)}, bf16[9,512,256]{2,1,0:T(8,128)(2,1)S(1)}) custom-call(f32[6]{0:T(128)S(1)} %stack.31.inside_ref, bf16[24,12,24,128]{3,2,1,0:T(8,128)(2,1)S(1)} %bitcast.25, bf16[24,24,128]{2,1,0:T(8,128)(2,1)S(1)} %collective-permute-done.1.layer_ref, bf16[24,16,128]{2,1,0:T(8,128)(2,1)S(1)} %get-tuple-element.51.below_ref, ...), custom_call_target="tpu_custom_call" | custom-call | flops 10000000000 | bytes 16777216 | tf_op jit(solution)/shard_map/windows/pallas_call | solution.py:220
  25.5 2.6 %collective-permute-done.6.refs_1_ = bf16[64,16,256]{2,1,0:T(8,128)(2,1)S(1)} collective-permute-done((bf16[64,16,256]{2,1,0:T(8,128)(2,1)S(1)}, bf16[64,16,256]{2,1,0:T(8,128)(2,1)S(1)}, u32[]{:S(2)}, u32[]{:S(2)}) %collective-permute-start.6) | collective-permute-done | bytes 524320 | tf_op jit(solution)/shard_map/ppermute | solution.py:540
  28.2 1.8 %collective-permute-start.8 = (bf16[64,16,256]{2,1,0:T(8,128)(2,1)S(1)}, bf16[64,16,256]{2,1,0:T(8,128)(2,1)S(1)}, u32[]{:S(2)}, u32[]{:S(2)}) collective-permute-start(bf16[64,16,256]{2,1,0:T(8,128)(2,1)S(1)} %collective-permute-done.6.refs_1_), channel_id=1, source_target_pairs={{0,2},{2,4},{4,6},{6,7},{7,5},{5,3},{3,1},{1,0},{8,10},{10,12},{12... | collective-permute-start | bytes 1572872 | tf_op jit(solution)/shard_map/ppermute | solution.py:540
  30.0 0.2 collective-permute-start.9
  30.2 10.1 %convolve.2.early_ref = bf16[16,224,256]{2,1,0:T(8,128)(2,1)S(1)} custom-call(bf16[6,6,224,768]{3,2,1,0:T(8,128)(2,1)S(1)} %get-tuple-element.29.first_ref.second_ref.third_ref, bf16[6,6,224,768]{3,2,1,0:T(8,128)(2,1)S(1)} %get-tuple-element.29.first_ref.second_ref.third_ref, bf16[6,6,224,768]{3,2,1,0:T(8,128)(2,1)S(1)} %get-tuple-element.29.first_ref.second_ref.third_ref, ...), custom_call_target="tpu_custom_call" | custom-call | flops 8455716864 | bytes 16777216 | tf_op jit(solution)/shard_map/convolve/pallas_call | solution.py:273
  40.3 0.0 copy-start.3
  40.3 0.0 collective-permute-done.8.refs_3_
  40.3 1.8 %collective-permute-start.10 = (bf16[64,16,256]{2,1,0:T(8,128)(2,1)S(1)}, bf16[64,16,256]{2,1,0:T(8,128)(2,1)S(1)}, u32[]{:S(2)}, u32[]{:S(2)}) collective-permute-start(bf16[64,16,256]{2,1,0:T(8,128)(2,1)S(1)} %collective-permute-done.8.refs_3_), channel_id=1, source_target_pairs={{0,2},{2,4},{4,6},{6,7},{7,5},{5,3},{3,1},{1,0},{8,10},{10,12},{12... | collective-permute-start | bytes 1572872 | tf_op jit(solution)/shard_map/ppermute | solution.py:540
  42.2 0.0 collective-permute-done.9.refs_4_
  42.2 0.2 collective-permute-start.11
  42.4 10.1 %convolve.3.late_ref = bf16[16,224,256]{2,1,0:T(8,128)(2,1)S(1)} custom-call(bf16[6,6,224,768]{3,2,1,0:T(8,128)(2,1)S(1)} %get-tuple-element.29.first_ref.second_ref.third_ref, bf16[6,6,224,768]{3,2,1,0:T(8,128)(2,1)S(1)} %get-tuple-element.29.first_ref.second_ref.third_ref, bf16[6,6,224,768]{3,2,1,0:T(8,128)(2,1)S(1)} %get-tuple-element.29.first_ref.second_ref.third_ref, ...), custom_call_target="tpu_custom_call" | custom-call | flops 8455716864 | bytes 16777216 | tf_op jit(solution)/shard_map/convolve/pallas_call | solution.py:273
  52.5 0.0 collective-permute-done.10.refs_5_
  52.5 1.8 %collective-permute-start.12 = (bf16[32,16,256]{2,1,0:T(8,128)(2,1)S(1)}, bf16[32,16,256]{2,1,0:T(8,128)(2,1)S(1)}, u32[]{:S(2)}, u32[]{:S(2)}) collective-permute-start(bf16[32,16,256]{2,1,0:T(8,128)(2,1)S(1)} %slice.33), channel_id=1, source_target_pairs={{0,2},{2,4},{4,6},{6,7},{7,5},{5,3},{3,1},{1,0},{8,10},{10,12},{12... | collective-permute-start | bytes 786440 | tf_op jit(solution)/shard_map/ppermute | solution.py:540
  54.4 0.0 collective-permute-done.11.refs_6_
  54.4 0.3 collective-permute-start.13
  54.7 4.3 %collective-permute-done.12.refs_7_ = bf16[32,16,256]{2,1,0:T(8,128)(2,1)S(1)} collective-permute-done((bf16[32,16,256]{2,1,0:T(8,128)(2,1)S(1)}, bf16[32,16,256]{2,1,0:T(8,128)(2,1)S(1)}, u32[]{:S(2)}, u32[]{:S(2)}) %collective-permute-start.12) | collective-permute-done | bytes 262176 | tf_op jit(solution)/shard_map/ppermute | solution.py:540
  59.0 1.9 %collective-permute-done.13.refs_8_ = bf16[32,16,256]{2,1,0:T(8,128)(2,1)S(1)} collective-permute-done((bf16[32,16,256]{2,1,0:T(8,128)(2,1)S(1)}, bf16[32,16,256]{2,1,0:T(8,128)(2,1)S(1)}, u32[]{:S(2)}, u32[]{:S(2)}) %collective-permute-start.13) | collective-permute-done | bytes 262176 | tf_op jit(solution)/shard_map/ppermute | solution.py:540
  60.8 1.1 %project.1 = bf16[224,256]{1,0:T(8,128)(2,1)S(1)} custom-call(s32[1]{0:T(128)} %bitcast.place_ref, bf16[16,224,256]{2,1,0:T(8,128)(2,1)S(1)} %convolve.2.early_ref, bf16[16,224,256]{2,1,0:T(8,128)(2,1)S(1)} %convolve.3.late_ref, bf16[64,16,256]{2,1,0:T(8,128)(2,1)S(1)} %regroup.1.refs_0_, bf16[64,16,256]{2,1,0:T(8,128)(2,1)S(1)} %collective-permute-done.6.refs_1_, ...), custom_call_target="tpu_custom_call" | custom-call | flops 939524096 | bytes 8388608 | tf_op jit(solution)/shard_map/project/pallas_call | solution.py:319
  62.0 0.3 collective-permute-start.14
  62.4 3.8 %collective-permute-done.14 = bf16[1,2,6,6,256]{4,3,2,1,0:T(8,128)(2,1)S(1)} collective-permute-done((bf16[1,2,6,6,256]{4,3,2,1,0:T(8,128)(2,1)S(1)}, bf16[1,2,6,6,256]{4,3,2,1,0:T(8,128)(2,1)S(1)}, u32[]{:S(2)}, u32[]{:S(2)}) %collective-permute-start.14) | collective-permute-done | bytes 36896 | tf_op jit(solution)/shard_map/ppermute | solution.py:477
  66.2 0.1 broadcast_select_fusion.4
  66.3 0.3 collective-permute-start.15
  66.6 0.1 broadcast_select_fusion.3
  66.7 1.8 %collective-permute-start.16 = (bf16[5,2,6,1,256]{4,3,2,1,0:T(2,128)(2,1)S(1)}, bf16[5,2,6,1,256]{4,3,2,1,0:T(2,128)(2,1)S(1)}, u32[]{:S(2)}, u32[]{:S(2)}) collective-permute-start(bf16[5,2,6,1,256]{4,3,2,1,0:T(2,128)(2,1)S(1)} %broadcast_select_fusion.3), channel_id=1, source_target_pairs={{0,2},{2,4},{4,6},{6,7},{7,5},{5,3},{3,1},{1,0},{8,10},{10,12},{12... | collective-permute-start | bytes 92168 | tf_op jit(solution)/shard_map/ppermute | solution.py:540
  69.2 1.4 %collective-permute-done.15 = bf16[5,2,6,1,256]{4,3,2,1,0:T(2,128)(2,1)S(1)} collective-permute-done((bf16[5,2,6,1,256]{4,3,2,1,0:T(2,128)(2,1)S(1)}, bf16[5,2,6,1,256]{4,3,2,1,0:T(2,128)(2,1)S(1)}, u32[]{:S(2)}, u32[]{:S(2)}) %collective-permute-start.15) | collective-permute-done | bytes 30752 | tf_op jit(solution)/shard_map/ppermute | solution.py:540
  70.6 0.4 collective-permute-done.16
  71.0 0.1 broadcast_select_fusion.5
  71.2 0.2 pad_maximum_fusion.field_ref
  71.4 4.5 %bottle_far.1 = (bf16[216,256]{1,0:T(8,128)(2,1)S(1)}, bf16[216,256]{1,0:T(8,128)(2,1)S(1)}) custom-call(s32[1]{0:T(128)} %bitcast.place_ref, bf16[5,2,8,8,256]{4,3,2,1,0:T(8,128)(2,1)S(1)} %pad_maximum_fusion.field_ref, bf16[27,256,1024]{2,1,0:T(8,128)(2,1)} %weight_ref.3), custom_call_target="tpu_custom_call" | custom-call | flops 2038431744 | bytes 8388608 | tf_op jit(solution)/shard_map/bottle_far/pallas_call | solution.py:406
  75.9 0.1 collective-permute-start.18
  76.0 0.0 copy-start.4
  76.0 1.9 %collective-permute-start.17 = (bf16[216,256]{1,0:T(8,128)(2,1)S(1)}, bf16[216,256]{1,0:T(8,128)(2,1)S(1)}, u32[]{:S(2)}, u32[]{:S(2)}) collective-permute-start(bf16[216,256]{1,0:T(8,128)(2,1)S(1)} %get-tuple-element.40), channel_id=1, source_target_pairs={{0,16},{8,24},{16,0},{24,8},{1,17},{9,25},{17,1},{25,9},{2,18},{10... | collective-permute-start | bytes 331784 | tf_op jit(solution)/shard_map/ppermute | solution.py:525
  77.8 4.6 %bottle_near.1 = (f32[216,256]{1,0:T(8,128)S(1)}, bf16[216,256]{1,0:T(8,128)(2,1)S(1)}) custom-call(s32[1]{0:T(128)} %bitcast.place_ref, bf16[5,2,8,8,256]{4,3,2,1,0:T(8,128)(2,1)S(1)} %pad_maximum_fusion.field_ref, bf16[27,256,1024]{2,1,0:T(8,128)(2,1)} %weight_ref.3), custom_call_target="tpu_custom_call" | custom-call | flops 2038431744 | bytes 8388608 | tf_op jit(solution)/shard_map/bottle_near/pallas_call | solution.py:406
  82.5 0.1 collective-permute-start.19
  82.6 1.1 %collective-permute-done.17 = bf16[216,256]{1,0:T(8,128)(2,1)S(1)} collective-permute-done((bf16[216,256]{1,0:T(8,128)(2,1)S(1)}, bf16[216,256]{1,0:T(8,128)(2,1)S(1)}, u32[]{:S(2)}, u32[]{:S(2)}) %collective-permute-start.17) | collective-permute-done | bytes 110624 | tf_op jit(solution)/shard_map/ppermute | solution.py:525
  83.7 0.1 collective-permute-done.19.refs_1_
  83.8 0.8 finish.1
  (30 shorter events, 0.3 us)
Async XLA Ops:
  0.0 1.0 %copy-start.2 = (bf16[256,1024]{1,0:T(8,128)(2,1)S(1)}, bf16[256,1024]{1,0:T(8,128)(2,1)}, u32[]{:S(2)}) copy-start(bf16[256,1024]{1,0:T(8,128)(2,1)} %rows_ref.1) | copy-start | bytes 1572868
  1.1 3.9 %collective-permute-start = (bf16[256,256]{1,0:T(8,128)(2,1)S(1)}, bf16[256,256]{1,0:T(8,128)(2,1)S(1)}, u32[]{:S(2)}, u32[]{:S(2)}) collective-permute-start(bf16[256,256]{1,0:T(8,128)(2,1)S(1)} %get-tuple-element.25), channel_id=1, source_target_pairs={{0,8},{8,0},{16,24},{24,16},{1,9},{9,1},{17,25},{25,17},{2,10},{10... | collective-permute-start | bytes 393224 | tf_op jit(solution)/shard_map/ppermute | solution.py:525
  1.6 12.7 %collective-permute-start.4 = (bf16[256,256]{1,0:T(8,128)(2,1)S(1)}, bf16[256,256]{1,0:T(8,128)(2,1)S(1)}, u32[]{:S(2)}, u32[]{:S(2)}) collective-permute-start(bf16[256,256]{1,0:T(8,128)(2,1)S(1)} %get-tuple-element.32), channel_id=1, source_target_pairs={{0,16},{8,24},{16,0},{24,8},{1,17},{9,25},{17,1},{25,9},{2,18},{10... | collective-permute-start | bytes 393224 | tf_op jit(solution)/shard_map/ppermute | solution.py:525
  4.2 10.2 %collective-permute-start.5 = (bf16[256,256]{1,0:T(8,128)(2,1)S(1)}, bf16[256,256]{1,0:T(8,128)(2,1)S(1)}, u32[]{:S(2)}, u32[]{:S(2)}) collective-permute-start(bf16[256,256]{1,0:T(8,128)(2,1)S(1)} %get-tuple-element.33), channel_id=1, source_target_pairs={{0,24},{8,16},{16,8},{24,0},{1,25},{9,17},{17,9},{25,1},{2,26},{10... | collective-permute-start | bytes 393224 | tf_op jit(solution)/shard_map/ppermute | solution.py:525
  5.9 4.1 %copy-start.8 = (f32[128]{0:T(128)S(1)}, f32[128]{0:T(128)}, u32[]{:S(2)}) copy-start(f32[128]{0:T(128)} %param.15) | copy-start | bytes 1540
  5.9 6.2 %collective-permute-start.1 = (bf16[24,24,128]{2,1,0:T(8,128)(2,1)S(1)}, bf16[24,24,128]{2,1,0:T(8,128)(2,1)S(1)}, u32[]{:S(2)}, u32[]{:S(2)}) collective-permute-start(bf16[24,24,128]{2,1,0:T(8,128)(2,1)S(1)} %dynamic-slice_bitcast_fusion), channel_id=1, source_target_pairs={{0,1},{1,0},{2,3},{3,2},{4,5},{5,4},{6,7},{7,6},{8,9},{9,8},{10,11... | collective-permute-start | bytes 442376 | tf_op jit(solution)/shard_map/ppermute | solution.py:477
  7.9 1.5 %copy-start = (bf16[1,24,24,12,128]{4,2,3,1,0:T(8,128)(2,1)S(1)}, bf16[1,24,24,12,128]{4,2,3,1,0:T(8,128)(2,1)}, u32[]{:S(2)}) copy-start(bf16[1,24,24,12,128]{4,2,3,1,0:T(8,128)(2,1)} %param.11) | copy-start | bytes 5308420
  9.4 10.0 %copy-start.5 = (bf16[3,3,3,128,128]{4,3,2,1,0:T(8,128)(2,1)S(1)}, bf16[3,3,3,128,128]{4,3,2,1,0:T(8,128)(2,1)}, u32[]{:S(2)}) copy-start(bf16[3,3,3,128,128]{4,3,2,1,0:T(8,128)(2,1)} %param.14) | copy-start | bytes 2654212
  10.0 9.4 %copy-start.1 = (bf16[1,24,24,12,128]{4,2,3,1,0:T(8,128)(2,1)S(1)}, bf16[1,24,24,12,128]{4,2,3,1,0:T(8,128)(2,1)}, u32[]{:S(2)}) copy-start(bf16[1,24,24,12,128]{4,2,3,1,0:T(8,128)(2,1)} %param.11) | copy-start | bytes 5308420
  10.0 9.4 %copy-start.6 = (f32[128]{0:T(128)S(1)}, f32[128]{0:T(128)}, u32[]{:S(2)}) copy-start(f32[128]{0:T(128)} %param.12) | copy-start | bytes 1540
  10.1 9.4 %copy-start.7 = (f32[128]{0:T(128)S(1)}, f32[128]{0:T(128)}, u32[]{:S(2)}) copy-start(f32[128]{0:T(128)} %param.13) | copy-start | bytes 1540
  12.3 4.9 %collective-permute-start.3 = (bf16[24,16,128]{2,1,0:T(8,128)(2,1)S(1)}, bf16[24,16,128]{2,1,0:T(8,128)(2,1)S(1)}, u32[]{:S(2)}, u32[]{:S(2)}) collective-permute-start(bf16[24,16,128]{2,1,0:T(8,128)(2,1)S(1)} %get-tuple-element.48), channel_id=1, source_target_pairs={{0,2},{2,4},{4,6},{6,7},{7,5},{5,3},{3,1},{1,0},{8,10},{10,12},{12... | collective-permute-start | bytes 294920 | tf_op jit(solution)/shard_map/ppermute | solution.py:540
  14.1 5.2 %collective-permute-start.2 = (bf16[24,16,128]{2,1,0:T(8,128)(2,1)S(1)}, bf16[24,16,128]{2,1,0:T(8,128)(2,1)S(1)}, u32[]{:S(2)}, u32[]{:S(2)}) collective-permute-start(bf16[24,16,128]{2,1,0:T(8,128)(2,1)S(1)} %get-tuple-element.49), channel_id=1, source_target_pairs={{2,0},{4,2},{6,4},{7,6},{5,7},{3,5},{1,3},{0,1},{10,8},{12,10},{14... | collective-permute-start | bytes 294920 | tf_op jit(solution)/shard_map/ppermute | solution.py:540
  15.0 13.1 %collective-permute-start.6 = (bf16[64,16,256]{2,1,0:T(8,128)(2,1)S(1)}, bf16[64,16,256]{2,1,0:T(8,128)(2,1)S(1)}, u32[]{:S(2)}, u32[]{:S(2)}) collective-permute-start(bf16[64,16,256]{2,1,0:T(8,128)(2,1)S(1)} %regroup.1.refs_0_), channel_id=1, source_target_pairs={{0,2},{2,4},{4,6},{6,7},{7,5},{5,3},{3,1},{1,0},{8,10},{10,12},{12... | collective-permute-start | bytes 1572872 | tf_op jit(solution)/shard_map/ppermute | solution.py:540
  16.9 13.1 %collective-permute-start.7 = (bf16[64,16,256]{2,1,0:T(8,128)(2,1)S(1)}, bf16[64,16,256]{2,1,0:T(8,128)(2,1)S(1)}, u32[]{:S(2)}, u32[]{:S(2)}) collective-permute-start(bf16[64,16,256]{2,1,0:T(8,128)(2,1)S(1)} %regroup.1.refs_0_), channel_id=1, source_target_pairs={{2,0},{4,2},{6,4},{7,6},{5,7},{3,5},{1,3},{0,1},{10,8},{12,10},{14... | collective-permute-start | bytes 1572872 | tf_op jit(solution)/shard_map/ppermute | solution.py:540
  28.2 12.2 %collective-permute-start.8 = (bf16[64,16,256]{2,1,0:T(8,128)(2,1)S(1)}, bf16[64,16,256]{2,1,0:T(8,128)(2,1)S(1)}, u32[]{:S(2)}, u32[]{:S(2)}) collective-permute-start(bf16[64,16,256]{2,1,0:T(8,128)(2,1)S(1)} %collective-permute-done.6.refs_1_), channel_id=1, source_target_pairs={{0,2},{2,4},{4,6},{6,7},{7,5},{5,3},{3,1},{1,0},{8,10},{10,12},{12... | collective-permute-start | bytes 1572872 | tf_op jit(solution)/shard_map/ppermute | solution.py:540
  30.0 12.2 %collective-permute-start.9 = (bf16[64,16,256]{2,1,0:T(8,128)(2,1)S(1)}, bf16[64,16,256]{2,1,0:T(8,128)(2,1)S(1)}, u32[]{:S(2)}, u32[]{:S(2)}) collective-permute-start(bf16[64,16,256]{2,1,0:T(8,128)(2,1)S(1)} %collective-permute-done.7.refs_2_), channel_id=1, source_target_pairs={{2,0},{4,2},{6,4},{7,6},{5,7},{3,5},{1,3},{0,1},{10,8},{12,10},{14... | collective-permute-start | bytes 1572872 | tf_op jit(solution)/shard_map/ppermute | solution.py:540
  40.3 20.5 %copy-start.3 = (f32[1024]{0:T(1024)S(1)}, f32[1024]{0:T(1024)}, u32[]{:S(2)}) copy-start(f32[1024]{0:T(1024)} %param.17) | copy-start | bytes 12292
  40.3 12.2 %collective-permute-start.10 = (bf16[64,16,256]{2,1,0:T(8,128)(2,1)S(1)}, bf16[64,16,256]{2,1,0:T(8,128)(2,1)S(1)}, u32[]{:S(2)}, u32[]{:S(2)}) collective-permute-start(bf16[64,16,256]{2,1,0:T(8,128)(2,1)S(1)} %collective-permute-done.8.refs_3_), channel_id=1, source_target_pairs={{0,2},{2,4},{4,6},{6,7},{7,5},{5,3},{3,1},{1,0},{8,10},{10,12},{12... | collective-permute-start | bytes 1572872 | tf_op jit(solution)/shard_map/ppermute | solution.py:540
  42.2 12.2 %collective-permute-start.11 = (bf16[64,16,256]{2,1,0:T(8,128)(2,1)S(1)}, bf16[64,16,256]{2,1,0:T(8,128)(2,1)S(1)}, u32[]{:S(2)}, u32[]{:S(2)}) collective-permute-start(bf16[64,16,256]{2,1,0:T(8,128)(2,1)S(1)} %collective-permute-done.9.refs_4_), channel_id=1, source_target_pairs={{2,0},{4,2},{6,4},{7,6},{5,7},{3,5},{1,3},{0,1},{10,8},{12,10},{14... | collective-permute-start | bytes 1572872 | tf_op jit(solution)/shard_map/ppermute | solution.py:540
  52.5 6.4 %collective-permute-start.12 = (bf16[32,16,256]{2,1,0:T(8,128)(2,1)S(1)}, bf16[32,16,256]{2,1,0:T(8,128)(2,1)S(1)}, u32[]{:S(2)}, u32[]{:S(2)}) collective-permute-start(bf16[32,16,256]{2,1,0:T(8,128)(2,1)S(1)} %slice.33), channel_id=1, source_target_pairs={{0,2},{2,4},{4,6},{6,7},{7,5},{5,3},{3,1},{1,0},{8,10},{10,12},{12... | collective-permute-start | bytes 786440 | tf_op jit(solution)/shard_map/ppermute | solution.py:540
  54.4 6.4 %collective-permute-start.13 = (bf16[32,16,256]{2,1,0:T(8,128)(2,1)S(1)}, bf16[32,16,256]{2,1,0:T(8,128)(2,1)S(1)}, u32[]{:S(2)}, u32[]{:S(2)}) collective-permute-start(bf16[32,16,256]{2,1,0:T(8,128)(2,1)S(1)} %slice.34), channel_id=1, source_target_pairs={{2,0},{4,2},{6,4},{7,6},{5,7},{3,5},{1,3},{0,1},{10,8},{12,10},{14... | collective-permute-start | bytes 786440 | tf_op jit(solution)/shard_map/ppermute | solution.py:540
  62.0 4.2 %collective-permute-start.14 = (bf16[1,2,6,6,256]{4,3,2,1,0:T(8,128)(2,1)S(1)}, bf16[1,2,6,6,256]{4,3,2,1,0:T(8,128)(2,1)S(1)}, u32[]{:S(2)}, u32[]{:S(2)}) collective-permute-start(bf16[1,2,6,6,256]{4,3,2,1,0:T(8,128)(2,1)S(1)} %select_n.176), channel_id=1, source_target_pairs={{0,1},{1,0},{2,3},{3,2},{4,5},{5,4},{6,7},{7,6},{8,9},{9,8},{10,11... | collective-permute-start | bytes 110600 | tf_op jit(solution)/shard_map/ppermute | solution.py:477
  66.3 4.3 %collective-permute-start.15 = (bf16[5,2,6,1,256]{4,3,2,1,0:T(2,128)(2,1)S(1)}, bf16[5,2,6,1,256]{4,3,2,1,0:T(2,128)(2,1)S(1)}, u32[]{:S(2)}, u32[]{:S(2)}) collective-permute-start(bf16[5,2,6,1,256]{4,3,2,1,0:T(2,128)(2,1)S(1)} %get-tuple-element.45), channel_id=1, source_target_pairs={{2,0},{4,2},{6,4},{7,6},{5,7},{3,5},{1,3},{0,1},{10,8},{12,10},{14... | collective-permute-start | bytes 92168 | tf_op jit(solution)/shard_map/ppermute | solution.py:540
  66.7 4.3 %collective-permute-start.16 = (bf16[5,2,6,1,256]{4,3,2,1,0:T(2,128)(2,1)S(1)}, bf16[5,2,6,1,256]{4,3,2,1,0:T(2,128)(2,1)S(1)}, u32[]{:S(2)}, u32[]{:S(2)}) collective-permute-start(bf16[5,2,6,1,256]{4,3,2,1,0:T(2,128)(2,1)S(1)} %broadcast_select_fusion.3), channel_id=1, source_target_pairs={{0,2},{2,4},{4,6},{6,7},{7,5},{5,3},{3,1},{1,0},{8,10},{10,12},{12... | collective-permute-start | bytes 92168 | tf_op jit(solution)/shard_map/ppermute | solution.py:540
  75.9 6.7 %collective-permute-start.18 = (bf16[216,256]{1,0:T(8,128)(2,1)S(1)}, bf16[216,256]{1,0:T(8,128)(2,1)S(1)}, u32[]{:S(2)}, u32[]{:S(2)}) collective-permute-start(bf16[216,256]{1,0:T(8,128)(2,1)S(1)} %get-tuple-element.41), channel_id=1, source_target_pairs={{0,24},{8,16},{16,8},{24,0},{1,25},{9,17},{17,9},{25,1},{2,26},{10... | collective-permute-start | bytes 331784 | tf_op jit(solution)/shard_map/ppermute | solution.py:525
  76.0 7.9 %copy-start.4 = (f32[1024]{0:T(1024)S(1)}, f32[1024]{0:T(1024)}, u32[]{:S(2)}) copy-start(f32[1024]{0:T(1024)} %param.19) | copy-start | bytes 12292
  76.0 7.7 %collective-permute-start.17 = (bf16[216,256]{1,0:T(8,128)(2,1)S(1)}, bf16[216,256]{1,0:T(8,128)(2,1)S(1)}, u32[]{:S(2)}, u32[]{:S(2)}) collective-permute-start(bf16[216,256]{1,0:T(8,128)(2,1)S(1)} %get-tuple-element.40), channel_id=1, source_target_pairs={{0,16},{8,24},{16,0},{24,8},{1,17},{9,25},{17,1},{25,9},{2,18},{10... | collective-permute-start | bytes 331784 | tf_op jit(solution)/shard_map/ppermute | solution.py:525
  82.5 1.4 %collective-permute-start.19 = (bf16[216,256]{1,0:T(8,128)(2,1)S(1)}, bf16[216,256]{1,0:T(8,128)(2,1)S(1)}, u32[]{:S(2)}, u32[]{:S(2)}) collective-permute-start(bf16[216,256]{1,0:T(8,128)(2,1)S(1)} %get-tuple-element.44), channel_id=1, source_target_pairs={{0,8},{8,0},{16,24},{24,16},{1,9},{9,1},{17,25},{25,17},{2,10},{10... | collective-permute-start | bytes 331784 | tf_op jit(solution)/shard_map/ppermute | solution.py:525
